TPU v7x, 128 devices: a whole 4x4x4 slice. The times are simulated.
128 devices in a mesh: dp: 32 (over z, x, y_lo), seq: 4 (over y_hi, core).
Axes of the slice: x: 4, y: 4 (y_hi: 2, y_lo: 2; y = y_hi * 2 + y_lo), z: 4, core: 2. Of those that a mesh axis runs over, the one named last changes fastest.
Arguments:
- clip_rows: bfloat16 [32768, 3072], P(('dp', 'seq')), may hold values from -24 to 24
- velocity_target: bfloat16 [32768, 3072], P(('dp', 'seq')), may hold values from -24 to 24
- plan: int32 [32, 4, 32], replicated, may hold values from 0 to 2, as said below
- segment_ids: int32 [32, 1024], P('dp'), may hold values from 0 to 1, as said below
- reward_levels: int32 [32, 2], P('dp'), may hold values from 1 to 8
- w_qkv: bfloat16 [3072, 4608], P('dp', 'seq'), may hold values from -0.109375 to 0.109375
- w_out: bfloat16 [3072, 1536], P('dp', 'seq'), may hold values from -0.15625 to 0.15625
Outputs:
- grad_qkv: float32 [3072, 4608], P('dp', 'seq')
- grad_out: float32 [3072, 1536], P('dp', 'seq')
Inputs may be any that keep to these rules, and one draw needn't show every extreme that they name: `plan`: for every g and s the counts over t sum to 32, and for every t and s the counts over g sum to 32; some count equals 2. `segment_ids`: in each group the rows before a boundary, which lies between 256 and 768, are piece 0 (the tail of an earlier clip) and the rest piece 1 (the start of the next clip).
All inputs are finite; a program needn't handle non-finite values.
Results may differ from a plain program's by a relative error of at most 0.03.
Values may be sent and summed in bfloat16 or wider, within the bound.
A program may use at most 128 MiB of HBM per device.

v0:
```python
import math

import jax
import jax.numpy as jnp
from jax import lax
from jax.sharding import PartitionSpec as P

HD = 128
CAP = 2


epsilon = 1e-06


def row_norm(values):
    factor = lax.rsqrt(jnp.mean(values * values, axis=-1, keepdims=True) + epsilon)
    return (values * factor, factor)


def per_device(clip_rows, velocity_target, plan, segment_ids, reward_levels, w_qkv, w_out):
    groups = lax.axis_size("dp")
    shards = lax.axis_size("seq")
    group = lax.axis_index("dp")
    shard = lax.axis_index("seq")
    rows_dev, width = clip_rows.shape
    block_rows = rows_dev // groups
    group_rows = rows_dev * shards
    counts = plan[group, shard]
    send_start = jnp.cumsum(counts) - counts
    slot_index = jnp.arange(CAP, dtype=jnp.int32)
    source_block = jnp.minimum(send_start[:, None] + slot_index[None, :], groups - 1).reshape(-1)
    occupied = (slot_index[None, :] < counts[:, None])[:, :, None, None]

    def pack(source_rows):
        blocks = source_rows.reshape(groups, block_rows, width)
        picked = jnp.take(blocks, source_block, axis=0).reshape(groups, CAP, block_rows, width)
        return jnp.where(occupied, picked, jnp.zeros((), source_rows.dtype))

    moved_rows, moved_target = (
        lax.all_to_all(pack(clip_rows), "dp", split_axis=0, concat_axis=0, tiled=True),
        lax.all_to_all(pack(velocity_target), "dp", split_axis=0, concat_axis=0, tiled=True),
    )
    arriving = plan[:, shard, group]
    arriving_end = jnp.cumsum(arriving)
    slot_ids = jnp.arange(groups, dtype=jnp.int32)
    source_group = jnp.sum((arriving_end[None, :] <= slot_ids[:, None]).astype(jnp.int32), axis=1)
    arriving_start = (arriving_end - arriving)[source_group]
    flat_slot = source_group * CAP + slot_ids - arriving_start

    def unpack(received):
        stacked = received.reshape(groups * CAP, block_rows, width)
        return jnp.take(stacked, flat_slot, axis=0).reshape(rows_dev, width)

    local_rows = unpack(moved_rows)
    local_target = unpack(moved_target)
    group_x, group_target = (
        lax.all_gather(local_rows, "seq", axis=0, tiled=True),
        lax.all_gather(local_target, "seq", axis=0, tiled=True),
    )
    qkv_full, out_full = (
        lax.all_gather(w_qkv, "dp", axis=0, tiled=True),
        lax.all_gather(w_out, "dp", axis=0, tiled=True),
    )
    projected = jnp.dot(group_x, qkv_full, preferred_element_type=jnp.float32)
    projected = projected.reshape(group_rows, -1, 3, HD)
    query_norm, query_factor = row_norm(projected[:, :, 0])
    key_norm, key_factor = row_norm(projected[:, :, 1])
    query_half = query_norm.astype(jnp.bfloat16)
    key_half = key_norm.astype(jnp.bfloat16)
    value_half = projected[:, :, 2].astype(jnp.bfloat16)
    local_heads = projected.shape[1]
    segment_row = segment_ids[0]
    same_segment = segment_row[:, None] == segment_row[None, :]
    scores = jnp.einsum(
        "qhe,khe->hqk", query_half, key_half, preferred_element_type=jnp.float32
    ) / math.sqrt(HD)
    expd = jnp.where(same_segment[None], jnp.exp(scores), jnp.float32(0.0))
    attention_probs = expd / jnp.sum(expd, axis=-1, keepdims=True)
    probs_half = attention_probs.astype(jnp.bfloat16)
    mixed = jnp.einsum("hqk,khe->qhe", probs_half, value_half, preferred_element_type=jnp.float32)
    mixed = mixed.astype(jnp.bfloat16).reshape(group_rows, local_heads * HD)
    partial_term = jnp.einsum("qc,dc->qd", mixed, out_full, preferred_element_type=jnp.float32)
    clip_index = jnp.arange(reward_levels.shape[1], dtype=jnp.int32)
    levels = reward_levels[0].astype(jnp.float32) / 8.0
    row_weight = jnp.sum(
        jnp.where(segment_row[:, None] == clip_index[None, :], levels[None, :], jnp.float32(0.0)),
        axis=1,
    )
    loss_scale = 1.0 / math.sqrt(rows_dev * groups * shards)
    summed = lax.psum(partial_term.astype(jnp.bfloat16), "seq").astype(jnp.float32)
    prediction = group_x.astype(jnp.float32) + summed
    pred_grad = (
        row_weight[:, None] * loss_scale * (prediction - group_target.astype(jnp.float32))
    ).astype(jnp.bfloat16)
    out_grad = jnp.dot(pred_grad, out_full, preferred_element_type=jnp.float32)
    out_grad = out_grad.astype(jnp.bfloat16).reshape(group_rows, local_heads, HD)
    value_grad = jnp.einsum(
        "hqk,qhe->khe", probs_half, out_grad, preferred_element_type=jnp.float32
    )
    prob_grad = jnp.einsum("qhe,khe->hqk", out_grad, value_half, preferred_element_type=jnp.float32)
    delta = jnp.sum(attention_probs * prob_grad, axis=-1, keepdims=True)
    score_grad = (attention_probs * (prob_grad - delta) / math.sqrt(HD)).astype(jnp.bfloat16)
    query_grad = jnp.einsum(
        "hqk,khe->qhe", score_grad, key_half, preferred_element_type=jnp.float32
    )
    key_grad = jnp.einsum(
        "hqk,qhe->khe", score_grad, query_half, preferred_element_type=jnp.float32
    )
    query_raw_grad = query_factor * (
        query_grad - query_norm * jnp.mean(query_grad * query_norm, axis=-1, keepdims=True)
    )
    key_raw_grad = key_factor * (
        key_grad - key_norm * jnp.mean(key_grad * key_norm, axis=-1, keepdims=True)
    )
    projected_grad = jnp.stack([query_raw_grad, key_raw_grad, value_grad], axis=2)
    projected_grad = projected_grad.reshape(group_rows, local_heads * 3 * HD).astype(jnp.bfloat16)
    qkv_part = jnp.einsum("qd,qc->dc", group_x, projected_grad, preferred_element_type=jnp.float32)
    out_part = jnp.einsum("qd,qc->dc", pred_grad, mixed, preferred_element_type=jnp.float32)
    summed_grads = lax.psum_scatter(
        jnp.concatenate([qkv_part, out_part], axis=1).astype(jnp.bfloat16),
        "dp",
        scatter_dimension=0,
        tiled=True,
    ).astype(jnp.float32)
    boundary = projected_grad.shape[1]
    return (summed_grads[:, :boundary], summed_grads[:, boundary:])


def solution(mesh):
    return jax.shard_map(
        per_device,
        mesh=mesh,
        in_specs=(
            P(("dp", "seq"), None),
            P(("dp", "seq"), None),
            P(),
            P("dp", None),
            P("dp", None),
            P("dp", "seq"),
            P("dp", "seq"),
        ),
        out_specs=(P("dp", "seq"), P("dp", "seq")),
        check_vma=False,
    )
```

profile of v0, /device:TPU:16, one launch (start us, length us, event | category | flops | bytes accessed | tf_op | source)
XLA Modules:
  0.0 1008.7 jit_solution(10563243071227993861)
XLA Ops:
  9.9 2.5 gather_fusion.1
  12.4 2.4 gather_fusion.3
  14.9 3.5 broadcast_select_fusion
  18.3 2.2 broadcast_select_fusion.2
  20.5 49.1 %all_to_all.10 = bf16[32,2,8,3072]{3,2,1,0:T(8,128)(2,1)} all-to-all(bf16[32,2,8,3072]{3,2,1,0:T(8,128)(2,1)S(1)} %get-tuple-element.19), channel_id=1, replica_groups=mesh['dp'=32,'seq'=4] {'dp'}, dimensions={0} | all-to-all | bytes 6291456 | tf_op jit(solution)/shard_map/all_to_all | solution.py:40
  69.6 4.8 all-to-all-start.1
  74.4 1.6 fusion.58
  77.1 2.5 gather_fusion.2
  79.6 36.5 %all-to-all-done.1 = bf16[32,2,8,3072]{3,2,1,0:T(8,128)(2,1)} async-done(((bf16[32,2,8,3072]{3,2,1,0:T(8,128)(2,1)}), bf16[32,2,8,3072]{3,2,1,0:T(8,128)(2,1)}, u32[]{:S(2)}, u32[]{:S(2)}) %all-to-all-start.1) | async-done | bytes 3145760 | tf_op jit(solution)/shard_map/all_to_all | solution.py:41
  116.1 2.5 gather_fusion.4
  118.7 2.0 select_bitcast_fusion
  122.8 1.7 broadcast_compare_fusion
  124.5 42.6 %all-gather.5.cloned.1.call-done = bf16[1024,3072]{1,0:T(8,128)(2,1)} async-done(((bf16[256,3072]{1,0:T(8,128)(2,1)}), bf16[1024,3072]{1,0:T(8,128)(2,1)}) %all-gather.5.cloned.1.call-update) | async-done | bytes 6291472 | tf_op jit(solution)/shard_map/all_gather | solution.py:57
  167.0 171.9 %all-gather.7.cloned.1.call-done = bf16[3072,1152]{1,0:T(8,128)(2,1)} async-done(((bf16[96,1152]{1,0:T(8,128)(2,1)}), bf16[3072,1152]{1,0:T(8,128)(2,1)}) %all-gather.7.cloned.1.call-update) | async-done | bytes 7077904 | tf_op jit(solution)/shard_map/all_gather | solution.py:61
  338.9 11.4 %fusion.64 = f32[1024,1152]{0,1:T(8,128)S(1)} fusion(bf16[1024,3072]{1,0:T(8,128)(2,1)} %all-gather.5.cloned.1.call-done, bf16[3072,1152]{1,0:T(8,128)(2,1)} %all-gather.7.cloned.1.call-done), kind=kOutput, calls=%fused_computation.89 | convolution fusion | flops 7247757312 | bytes 18087936 | tf_op jit(solution)/shard_map/dot_general | solution.py:64
  352.4 6.2 fusion.3
  358.6 7.6 fusion.24
  366.2 127.5 %all-gather.9.cloned.1.call-done = bf16[3072,384]{1,0:T(8,128)(2,1)} async-done(((bf16[96,384]{1,0:T(8,128)(2,1)}), bf16[3072,384]{1,0:T(8,128)(2,1)}) %all-gather.9.cloned.1.call-update) | async-done | bytes 2359312 | tf_op jit(solution)/shard_map/all_gather | solution.py:62
  493.7 8.1 convolution_convert_fusion.1
  502.6 40.3 %all-gather.11.cloned.1.call-done = bf16[1024,3072]{1,0:T(8,128)(2,1)} async-done(((bf16[256,3072]{1,0:T(8,128)(2,1)}), bf16[1024,3072]{1,0:T(8,128)(2,1)}) %all-gather.11.cloned.1.call-update) | async-done | bytes 6291472 | tf_op jit(solution)/shard_map/all_gather | solution.py:58
  542.8 128.6 %all-reduce.2.cloned.1.call-done = bf16[1024,3072]{1,0:T(8,128)(2,1)} async-done(((bf16[1024,3072]{1,0:T(8,128)(2,1)}), bf16[1024,3072]{1,0:T(8,128)(2,1)}) %all-reduce.2.cloned.1.call-update) | async-done | bytes 6291472 | tf_op jit(solution)/shard_map/psum | solution.py:90
  671.4 8.9 multiply_convert_fusion.1
  680.3 2.7 convolution_convert_fusion.3
  683.9 7.7 fusion.38
  691.7 21.5 %fusion.19 = (f32[1024,3]{0,1:T(4,128)S(1)}, f32[3,128,1024]{2,1,0:T(8,128)}) fusion(f32[1024,3,1,128]{0,3,2,1:T(8,128)S(1)} %get-tuple-element.17, f32[1024,3]{0,1:T(4,128)S(1)} %add_rsqrt_fusion.1, f32[3,1024,1024]{1,2,0:T(8,128)} %fusion.38, f32[3,1024]{1,0:T(4,128)S(1)} %get-tuple-element.24, f32[3,1024,1024]{1,2,0:T(8,128)} %get-tuple-element.25, ...), kind=kOutput, calls=%fused_computation.39 | convolution fusion | flops 841876480 | bytes 30982144 | tf_op jit(solution)/shard_map/hqk,khe->qhe/dot_general | solution.py:103
  713.1 20.4 %fusion.16 = (f32[1024,3]{0,1:T(4,128)S(1)}, f32[3,128,1024]{2,1,0:T(8,128)}) fusion(f32[1024,3,1,128]{0,3,2,1:T(8,128)S(1)} %get-tuple-element.16, f32[1024,3]{0,1:T(4,128)S(1)} %add_rsqrt_fusion, f32[3,1024,1024]{1,2,0:T(8,128)} %fusion.38, f32[3,1024]{1,0:T(4,128)S(1)} %get-tuple-element.24, f32[3,1024,1024]{1,2,0:T(8,128)} %get-tuple-element.25, ...), kind=kOutput, calls=%fused_computation.34 | convolution fusion | flops 841876480 | bytes 30982144 | tf_op jit(solution)/shard_map/hqk,qhe->khe/dot_general | solution.py:106
  733.5 8.7 fusion.30
  742.2 5.8 convolution_convert_fusion.2
  752.4 7.9 convolution_convert_fusion
  760.3 10.4 %pad_maximum_fusion = bf16[3072,1536]{0,1:T(8,128)(2,1)} fusion(bf16[3072,384]{0,1:T(8,128)(2,1)S(1)} %convolution_convert_fusion.2, bf16[3072,1152]{0,1:T(8,128)(2,1)S(1)} %convolution_convert_fusion), kind=kLoop, calls=%fused_computation.14 | loop fusion | flops 18874368 | bytes 18874368 | tf_op jit(solution)/shard_map/concatenate | solution.py:120
  770.7 12.7 %copy.84 = bf16[3072,1536]{1,0:T(8,128)(2,1)} copy(bf16[3072,1536]{0,1:T(8,128)(2,1)} %pad_maximum_fusion) | data formatting | bytes 18874368
  783.4 213.8 %reduce-scatter.4.cloned.1.call-done = bf16[96,1536]{1,0:T(8,128)(2,1)} async-done(((bf16[3072,1536]{1,0:T(8,128)(2,1)}), bf16[96,1536]{1,0:T(8,128)(2,1)}) %reduce-scatter.4.cloned.1.call-update) | async-done | bytes 294928
  (83 shorter events, 17.8 us)
Async XLA Ops:
  7.2 2.7 copy-start
  7.2 5.2 copy-start.2
  69.6 46.6 %all-to-all-start.1 = ((bf16[32,2,8,3072]{3,2,1,0:T(8,128)(2,1)}), bf16[32,2,8,3072]{3,2,1,0:T(8,128)(2,1)}, u32[]{:S(2)}, u32[]{:S(2)}) async-start(bf16[32,2,8,3072]{3,2,1,0:T(8,128)(2,1)} %get-tuple-element.18), calls=%async_computation.1 | async-start | bytes 6291456 | tf_op jit(solution)/shard_map/all_to_all | solution.py:41
  74.4 92.6 %all-gather.5.cloned.1.call-start = ((), (), s32[]{:S(2)}) async-start(), calls=%async_computation.3 | async-start | bytes 7864320 | tf_op jit(solution)/shard_map/all_gather | solution.py:57
  118.7 4.2 copy-start.9
  120.7 218.2 %all-gather.7.cloned.1.call-start = ((), (), s32[]{:S(2)}) async-start(), calls=%async_computation.4 | async-start | bytes 7299072 | tf_op jit(solution)/shard_map/all_gather | solution.py:61
  121.5 372.2 %all-gather.9.cloned.1.call-start = ((), (), s32[]{:S(2)}) async-start(), calls=%async_computation.5 | async-start | bytes 2433024 | tf_op jit(solution)/shard_map/all_gather | solution.py:62
  122.2 420.7 %all-gather.11.cloned.1.call-start = ((), (), s32[]{:S(2)}) async-start(), calls=%async_computation.7 | async-start | bytes 7864320 | tf_op jit(solution)/shard_map/all_gather | solution.py:58
  122.8 548.6 %all-reduce.2.cloned.1.call-start = ((), (), s32[]{:S(2)}) async-start(), calls=%async_computation.6 | async-start | bytes 12582912 | tf_op jit(solution)/shard_map/psum | solution.py:90
  350.4 8.3 copy-start.4
  350.4 2.0 copy-start.8
  501.8 0.7 copy-start.11
  501.8 495.5 %reduce-scatter.4.cloned.1.call-start = ((), (), s32[]{:S(2)}) async-start(), calls=%async_computation.8 | async-start | bytes 9732096
  671.4 8.9 copy-start.10
  680.3 2.7 copy-start.3
  683.1 0.9 copy-start.7
  733.5 8.7 copy-start.12
  742.2 5.8 copy-start.6
  748.0 1.4 copy-start.5
  749.4 2.2 slice-start
  749.8 2.6 slice-start.1
  783.4 217.9 %copy-start.1 = (bf16[256,3072]{1,0:T(8,128)(2,1)S(1)}, bf16[256,3072]{1,0:T(8,128)(2,1)}, u32[]{:S(2)}) copy-start(bf16[256,3072]{1,0:T(8,128)(2,1)} %param.11) | copy-start | bytes 4718596
Sparse Core Ops, SparseCore 0:
  120.8 46.1 all-gather.4
  168.7 170.1 all-gather.6
  340.6 153.1 all-gather.8
  495.2 47.5 all-gather.10
  545.2 126.1 all-reduce.1
  783.6 213.6 reduce-scatter.3
where the time goes:
time: 1010 us
  waiting for transfers between devices  763 us (76%)
  matrix products  108 us (11%)
  blocking collectives  49.1 us (5%)
  local copies, waits for them, and re-layouts  37 us (4%)
  other arithmetic  31.5 us (3%)
  between operations  15 us (1%)
    unnamed x7, waiting for transfers between devices  216 us
    all_gather x1, waiting for transfers between devices, per_device(): lax.all_gather(w_qkv, 'dp', axis=0, tiled=True)  172 us
    psum x1, waiting for transfers between devices, per_device(): lax.psum(partial_term.astype(jnp.bfloat16), 'seq').astype(jnp.float32)  129 us
    all_gather x1, waiting for transfers between devices, per_device(): lax.all_gather(w_out, 'dp', axis=0, tiled=True)  127 us
    all_to_all x1, blocking collectives, per_device(): lax.all_to_all(pack(clip_rows), 'dp', split_axis=0, concat_axis=0, tiled=...  49.1 us
    all_gather x1, waiting for transfers between devices, per_device(): lax.all_gather(local_rows, 'seq', axis=0, tiled=True)  42.6 us
    all_gather x1, waiting for transfers between devices, per_device(): lax.all_gather(local_target, 'seq', axis=0, tiled=True)  40.3 us
    all_to_all x1, waiting for transfers between devices, per_device(): lax.all_to_all(pack(velocity_target), 'dp', split_axis=0, concat_axis=0,...  36.5 us
  transfers between devices with their start and end apart: 7, of which 7 were waited for; matrix products, arithmetic and copies ran while one was open for 4% of the time, Pallas kernels for 0%

commit v1 on v0

v1 whole, which is shorter than its diff:
```python
import math

import jax
import jax.numpy as jnp
from jax import lax
from jax.experimental import pallas as pl
from jax.experimental.pallas import tpu as pltpu
from jax.sharding import PartitionSpec as P

HD = 128
CAP = 2
MESH = pl.DeviceIdType.MESH
VMEM_LIMIT = 60 * 1024 * 1024

epsilon = 1e-06


def my_place():
    dp = lax.axis_index("dp")
    seq = lax.axis_index("seq")
    return (dp // 8, (dp // 2) % 4, dp % 2, seq // 2, seq % 2)


def device(place):
    z, x, y, a, c = place
    return {"dp": z * 8 + x * 2 + y, "seq": a * 2 + c}


def moved(place, axis, by):
    place = list(place)
    size = (4, 4, 2, 2, 2)[axis]
    place[axis] = (place[axis] + by + size) % size
    return tuple(place)


Z, X, Y, A, C = range(5)


class Copies:
    def __init__(self, send_sem, recv_sem):
        self.send_sem, self.recv_sem, self.used = send_sem, recv_sem, 0
        self.started = []

    def start(self, src, dst, to):
        copy = pltpu.make_async_remote_copy(
            src_ref=src,
            dst_ref=dst,
            send_sem=self.send_sem.at[self.used],
            recv_sem=self.recv_sem.at[self.used],
            device_id=device(to),
            device_id_type=MESH,
        )
        self.used += 1
        copy.start()
        self.started.append(copy)
        return copy

    def finish(self):
        for copy in self.started:
            copy.wait_send()


def greet(places):
    barrier = pltpu.get_barrier_semaphore()
    for place in places:
        pl.semaphore_signal(barrier, inc=1, device_id=device(place), device_id_type=MESH)
    pl.semaphore_wait(barrier, len(places))


def dp_peer(place, k, sign):
    z, x, y, a, c = place
    dz, dx, dy = k // 8, (k // 2) % 4, k % 2
    return ((z + sign * dz + 4) % 4, (x + sign * dx + 4) % 4, (y + sign * dy + 2) % 2, a, c)


def ring_gather_start(copies, me, axis, part):
    own = me[axis]
    up, down = moved(me, axis, 1), moved(me, axis, -1)
    first_up = copies.start(part(own, 0), part(own, 0), up)
    first_down = copies.start(part(own, 1), part(own, 1), down)
    second_up = copies.start(part(own, 1), part(own, 1), up)
    second_down = copies.start(part(own, 0), part(own, 0), down)
    return first_up, first_down, second_up, second_down


def ring_gather_forward(copies, me, axis, part, sent):
    up, down = moved(me, axis, 1), moved(me, axis, -1)
    below, above = down[axis], up[axis]
    sent[0].wait_recv()
    third_up = copies.start(part(below, 0), part(below, 0), up)
    sent[1].wait_recv()
    third_down = copies.start(part(above, 1), part(above, 1), down)
    return sent[2], sent[3], third_up, third_down


def gather_kernel(packed, shard, chosen, x_full, w_full, received, own_rows, a2a_send, a2a_recv, send_sem, recv_sem, local_sem):
    me = my_place()
    z, x, y, a, c = me
    dp = lax.axis_index("dp")
    seq = lax.axis_index("seq")
    rows = own_rows.shape[0]
    other_chip, other_core = moved(me, A, 1), moved(me, C, 1)
    barrier = pltpu.get_barrier_semaphore()

    @pl.loop(1, 32)
    def _(k):
        pl.semaphore_signal(barrier, inc=1, device_id=device(dp_peer(me, k, 1)), device_id_type=MESH)

    for place in (other_chip, other_core):
        pl.semaphore_signal(barrier, inc=1, device_id=device(place), device_id_type=MESH)
    pl.semaphore_wait(barrier, 33)

    copies = Copies(send_sem, recv_sem)
    own_shard = pltpu.make_async_copy(shard, w_full.at[z, x, y], local_sem.at[0])
    own_shard.start()
    across = copies.start(shard, w_full.at[z, x, y], moved(me, Y, 1))

    def block_copy(k):
        to = dp_peer(me, k, 1)
        return pltpu.make_async_remote_copy(
            src_ref=packed.at[device(to)["dp"]],
            dst_ref=received.at[dp],
            send_sem=a2a_send.at[k],
            recv_sem=a2a_recv.at[k],
            device_id=device(to),
            device_id_type=MESH,
        )

    @pl.loop(1, 32)
    def _(k):
        block_copy(k).start()

    own_block = pltpu.make_async_copy(packed.at[dp], received.at[dp], local_sem.at[1])
    own_block.start()

    own_shard.wait()
    across.wait_recv()

    def near(half):
        if half == 0:
            return lambda at, which: w_full.at[at, x, which, 0]
        return lambda at, which: w_full.at[z, at, which, 1]

    def far(half):
        if half == 0:
            return lambda at, which: w_full.at[pl.ds(2 * which, 2), at, :, 0]
        return lambda at, which: w_full.at[at, pl.ds(2 * which, 2), :, 1]

    near_axis, far_axis = (Z, X), (X, Z)
    sent = [ring_gather_start(copies, me, near_axis[half], near(half)) for half in (0, 1)]
    rest = [ring_gather_forward(copies, me, near_axis[half], near(half), sent[half]) for half in (0, 1)]
    for half in (0, 1):
        for copy in rest[half]:
            copy.wait_recv()
    sent = [ring_gather_start(copies, me, far_axis[half], far(half)) for half in (0, 1)]

    own_block.wait()

    @pl.loop(1, 32)
    def _(k):
        block_copy(k).wait_recv()

    width = own_rows.shape[1]
    tile = 512

    @pl.loop(0, width // tile)
    def _(t):
        columns = pl.ds(pl.multiple_of(t * tile, tile), tile)
        blocks = received[:, :, columns].reshape(rows * CAP, tile)
        own_rows[:, columns] = jnp.dot(chosen[...], blocks, preferred_element_type=jnp.float32).astype(jnp.bfloat16)

    def rows_of(place):
        return pl.ds(pl.multiple_of(device(place)["seq"] * rows, rows), rows)

    to_chip = copies.start(own_rows, x_full.at[rows_of(me)], other_chip)
    to_core = copies.start(own_rows, x_full.at[rows_of(me)], other_core)
    own_place = pltpu.make_async_copy(own_rows, x_full.at[rows_of(me)], local_sem.at[2])
    own_place.start()

    rest = [ring_gather_forward(copies, me, far_axis[half], far(half), sent[half]) for half in (0, 1)]
    to_chip.wait_recv()
    passed = copies.start(x_full.at[rows_of(other_chip)], x_full.at[rows_of(other_chip)], other_core)
    to_core.wait_recv()
    passed.wait_recv()
    for half in (0, 1):
        for copy in rest[half]:
            copy.wait_recv()
    own_place.wait()

    @pl.loop(1, 32)
    def _(k):
        block_copy(k).wait_send()

    copies.finish()


def gather_all(packed, shard, chosen):
    rows = chosen.shape[0]
    width = packed.shape[2]
    w_cols = shard.shape[1]
    x_full, w_full = pl.pallas_call(
        gather_kernel,
        out_shape=(
            jax.ShapeDtypeStruct((rows * 4, width), jnp.bfloat16),
            jax.ShapeDtypeStruct((4, 4, 2, 2, 48, w_cols), jnp.bfloat16),
        ),
        in_specs=[
            pl.BlockSpec(memory_space=pl.ANY),
            pl.BlockSpec(memory_space=pl.ANY),
            pl.BlockSpec(memory_space=pltpu.VMEM),
        ],
        out_specs=(pl.BlockSpec(memory_space=pl.ANY), pl.BlockSpec(memory_space=pl.ANY)),
        scratch_shapes=[
            pltpu.VMEM(packed.shape, jnp.bfloat16),
            pltpu.VMEM((rows, width), jnp.bfloat16),
            pltpu.SemaphoreType.DMA((32,)),
            pltpu.SemaphoreType.DMA((32,)),
            pltpu.SemaphoreType.DMA((28,)),
            pltpu.SemaphoreType.DMA((28,)),
            pltpu.SemaphoreType.DMA((3,)),
        ],
        compiler_params=pltpu.CompilerParams(collective_id=1, has_side_effects=True, vmem_limit_bytes=VMEM_LIMIT),
        name="gather_rows_weights",
    )(packed, shard.reshape(2, 48, w_cols), chosen)
    return x_full, w_full.reshape(3072, w_cols)


CHUNKS = 4


def residual_kernel(packed, chosen, partial, x_own, weight, d_full, received, target, from_core, summed, from_chip, a2a_send, a2a_recv, send_sem, recv_sem, local_sem):
    me = my_place()
    dp = lax.axis_index("dp")
    rows, width = x_own.shape
    other_chip, other_core = moved(me, A, 1), moved(me, C, 1)
    barrier = pltpu.get_barrier_semaphore()

    @pl.loop(1, 32)
    def _(k):
        pl.semaphore_signal(barrier, inc=1, device_id=device(dp_peer(me, k, 1)), device_id_type=MESH)

    for place in (other_chip, other_core):
        pl.semaphore_signal(barrier, inc=1, device_id=device(place), device_id_type=MESH)
    pl.semaphore_wait(barrier, 33)

    copies = Copies(send_sem, recv_sem)
    step = rows // CHUNKS

    def rows_of(place, chunk):
        return pl.ds(pl.multiple_of(device(place)["seq"] * rows + chunk * step, step), step)

    core_first, core_second = [], []
    for chunk in range(CHUNKS):
        core_first.append(copies.start(
            partial.at[rows_of(moved(other_core, A, 1), chunk)], from_core.at[0, pl.ds(chunk * step, step)], other_core))
    for chunk in range(CHUNKS):
        core_second.append(copies.start(
            partial.at[rows_of(other_core, chunk)], from_core.at[1, pl.ds(chunk * step, step)], other_core))

    def block_copy(k):
        to = dp_peer(me, k, 1)
        return pltpu.make_async_remote_copy(
            src_ref=packed.at[device(to)["dp"]],
            dst_ref=received.at[dp],
            send_sem=a2a_send.at[k],
            recv_sem=a2a_recv.at[k],
            device_id=device(to),
            device_id_type=MESH,
        )

    @pl.loop(1, 32)
    def _(k):
        block_copy(k).start()

    own_block = pltpu.make_async_copy(packed.at[dp], received.at[dp], local_sem.at[0])
    own_block.start()

    chip_sums = []
    for chunk in range(CHUNKS):
        core_first[chunk].wait_recv()
        at = pl.ds(chunk * step, step)
        summed[at] = (partial[rows_of(other_chip, chunk)].astype(jnp.float32) + from_core[0, at].astype(jnp.float32)).astype(jnp.bfloat16)
        chip_sums.append(copies.start(summed.at[at], from_chip.at[at], other_chip))

    own_block.wait()

    @pl.loop(1, 32)
    def _(k):
        block_copy(k).wait_recv()

    tile = 512

    @pl.loop(0, width // tile)
    def _(t):
        columns = pl.ds(pl.multiple_of(t * tile, tile), tile)
        blocks = received[:, :, columns].reshape(rows * CAP, tile)
        target[:, columns] = jnp.dot(chosen[...], blocks, preferred_element_type=jnp.float32).astype(jnp.bfloat16)

    to_chip, to_core, passed = [], [], []
    for chunk in range(CHUNKS):
        core_second[chunk].wait_recv()
        chip_sums[chunk].wait_recv()
        at = pl.ds(chunk * step, step)
        mine = rows_of(me, chunk)
        prediction = (
            x_own[at].astype(jnp.float32)
            + (partial[mine].astype(jnp.float32) + from_core[1, at].astype(jnp.float32) + from_chip[at].astype(jnp.float32))
        )
        d_full[mine] = (weight[at] * (prediction - target[at].astype(jnp.float32))).astype(jnp.bfloat16)
        to_chip.append(copies.start(d_full.at[mine], d_full.at[mine], other_chip))
        to_core.append(copies.start(d_full.at[mine], d_full.at[mine], other_core))
    for chunk in range(CHUNKS):
        to_chip[chunk].wait_recv()
        theirs = rows_of(other_chip, chunk)
        passed.append(copies.start(d_full.at[theirs], d_full.at[theirs], other_core))
    for chunk in range(CHUNKS):
        to_core[chunk].wait_recv()
        passed[chunk].wait_recv()

    @pl.loop(1, 32)
    def _(k):
        block_copy(k).wait_send()

    copies.finish()


def residual(packed, chosen, partial, x_own, weight):
    rows, width = x_own.shape
    return pl.pallas_call(
        residual_kernel,
        out_shape=jax.ShapeDtypeStruct(partial.shape, jnp.bfloat16),
        in_specs=[pl.BlockSpec(memory_space=pl.ANY)] + [pl.BlockSpec(memory_space=pltpu.VMEM)] * 4,
        out_specs=pl.BlockSpec(memory_space=pltpu.VMEM),
        scratch_shapes=[
            pltpu.VMEM(packed.shape, jnp.bfloat16),
            pltpu.VMEM((rows, width), jnp.bfloat16),
            pltpu.VMEM((2, rows, width), jnp.bfloat16),
            pltpu.VMEM((rows, width), jnp.bfloat16),
            pltpu.VMEM((rows, width), jnp.bfloat16),
            pltpu.SemaphoreType.DMA((32,)),
            pltpu.SemaphoreType.DMA((32,)),
            pltpu.SemaphoreType.DMA((6 * CHUNKS,)),
            pltpu.SemaphoreType.DMA((6 * CHUNKS,)),
            pltpu.SemaphoreType.DMA((1,)),
        ],
        compiler_params=pltpu.CompilerParams(collective_id=2, has_side_effects=True, vmem_limit_bytes=VMEM_LIMIT),
        name="residual_gradient",
    )(packed, chosen, partial, x_own, weight)


def added(*values):
    total = values[0].astype(jnp.float32)
    for value in values[1:]:
        total = total + value.astype(jnp.float32)
    return total


def reduce_start(copies, me, axis, block, got):
    up, down = moved(me, axis, 1), moved(me, axis, -1)
    opposite = moved(me, axis, 2)[axis]
    far_up = copies.start(block(opposite, 0), got(0), up)
    far_down = copies.start(block(opposite, 1), got(1), down)
    near_up = copies.start(block(up[axis], 1), got(2), up)
    near_down = copies.start(block(down[axis], 0), got(3), down)
    return far_up, far_down, near_up, near_down


def reduce_pass(copies, me, axis, block, got, sums, sent, add):
    up, down = moved(me, axis, 1), moved(me, axis, -1)
    sent[0].wait_recv()
    add(sums(0), [block(up[axis], 0), got(0)])
    sum_up = copies.start(sums(0), got(4), up)
    sent[1].wait_recv()
    add(sums(1), [block(down[axis], 1), got(1)])
    sum_down = copies.start(sums(1), got(5), down)
    return sent[2], sent[3], sum_up, sum_down


def reduce_end(me, axis, block, got, out, sent, add):
    sent[1].wait_recv()
    sent[2].wait_recv()
    add(out(0), [block(me[axis], 0), got(3), got(4)])
    sent[0].wait_recv()
    sent[3].wait_recv()
    add(out(1), [block(me[axis], 1), got(2), got(5)])


def add_rows(out, parts):
    lead = out.shape[:-2]
    count = math.prod(lead)

    @pl.loop(0, count)
    def _(i):
        index, rest = [], i
        for size in reversed(lead):
            index.insert(0, rest % size)
            rest = rest // size
        index = tuple(index)
        out[index] = added(*[part[index] for part in parts]).astype(out.dtype)


def scatter_kernel(grads, sums_out, got_far, sum_far, half_far, got_near, sum_near, half_near, got_last, send_sem, recv_sem):
    me = my_place()
    z, x, y, a, c = me
    greet([moved(me, Z, 1), moved(me, Z, -1), moved(me, X, 1), moved(me, X, -1), moved(me, Y, 1)])
    copies = Copies(send_sem, recv_sem)
    far_axis, near_axis = (X, Z), (Z, X)

    def far_block(half):
        if half == 0:
            return lambda at, which: grads.at[pl.ds(2 * which, 2), at, :, 0]
        return lambda at, which: grads.at[at, pl.ds(2 * which, 2), :, 1]

    def near_block(half):
        return lambda at, which: half_far.at[half, at, which]

    def slots(ref, half):
        return lambda j: ref.at[half, j]

    def far_out(half):
        return lambda which: half_far.at[half, pl.ds(2 * which, 2)]

    def near_out(half):
        return lambda which: half_near.at[half, pl.ds(which, 1)]

    def near_add(out, parts):
        out[...] = added(*[part[...] for part in parts]).astype(out.dtype).reshape(out.shape)

    sent = [reduce_start(copies, me, far_axis[h], far_block(h), slots(got_far, h)) for h in (0, 1)]
    sent = [reduce_pass(copies, me, far_axis[h], far_block(h), slots(got_far, h), slots(sum_far, h), sent[h], add_rows) for h in (0, 1)]
    for h in (0, 1):
        reduce_end(me, far_axis[h], far_block(h), slots(got_far, h), far_out(h), sent[h], add_rows)
    sent = [reduce_start(copies, me, near_axis[h], near_block(h), slots(got_near, h)) for h in (0, 1)]
    sent = [reduce_pass(copies, me, near_axis[h], near_block(h), slots(got_near, h), slots(sum_near, h), sent[h], near_add) for h in (0, 1)]
    for h in (0, 1):
        reduce_end(me, near_axis[h], near_block(h), slots(got_near, h), near_out(h), sent[h], near_add)
    last = [copies.start(half_near.at[h, 1 - y], got_last.at[h], moved(me, Y, 1)) for h in (0, 1)]
    for h in (0, 1):
        last[h].wait_recv()
        sums_out[h] = added(half_near[h, y], got_last[h])
    copies.finish()


def scatter(grads):
    cols = grads.shape[1]
    half = lambda *lead: pltpu.VMEM((2, *lead, 48, cols), jnp.bfloat16)
    sums = pl.pallas_call(
        scatter_kernel,
        out_shape=jax.ShapeDtypeStruct((2, 48, cols), jnp.float32),
        in_specs=[pl.BlockSpec(memory_space=pltpu.VMEM)],
        out_specs=pl.BlockSpec(memory_space=pltpu.VMEM),
        scratch_shapes=[
            half(6, 2, 2),
            half(2, 2, 2),
            half(4, 2),
            half(6),
            half(2),
            half(2),
            half(),
            pltpu.SemaphoreType.DMA((26,)),
            pltpu.SemaphoreType.DMA((26,)),
        ],
        compiler_params=pltpu.CompilerParams(collective_id=3, has_side_effects=True, vmem_limit_bytes=VMEM_LIMIT),
        name="scatter_gradients",
    )(grads.reshape(4, 4, 2, 2, 48, cols))
    return sums.reshape(96, cols)


def row_norm(values):
    factor = lax.rsqrt(jnp.mean(values * values, axis=-1, keepdims=True) + epsilon)
    return (values * factor, factor)


def spread(block_of, rows, columns):
    source = jnp.repeat(block_of, 8) * 8 + jnp.tile(jnp.arange(8, dtype=jnp.int32), rows // 8)
    source = jnp.where(jnp.repeat(block_of, 8) < 0, -1, source)
    return (source[:, None] == jnp.arange(columns, dtype=jnp.int32)[None, :]).astype(jnp.bfloat16)


def per_device(clip_rows, velocity_target, plan, segment_ids, reward_levels, w_qkv, w_out):
    groups = lax.axis_size("dp")
    shards = lax.axis_size("seq")
    group = lax.axis_index("dp")
    shard = lax.axis_index("seq")
    rows_dev, width = clip_rows.shape
    group_rows = rows_dev * shards
    counts = plan[group, shard]
    send_start = jnp.cumsum(counts) - counts
    slot_index = jnp.arange(CAP, dtype=jnp.int32)
    source_block = jnp.where(slot_index[None, :] < counts[:, None], send_start[:, None] + slot_index[None, :], -1).reshape(-1)
    pack = spread(source_block, rows_dev * CAP, rows_dev)

    def packed(source_rows):
        return jnp.dot(pack, source_rows, preferred_element_type=jnp.float32).astype(jnp.bfloat16).reshape(groups, CAP * 8, width)

    arriving = plan[:, shard, group]
    arriving_end = jnp.cumsum(arriving)
    slot_ids = jnp.arange(groups, dtype=jnp.int32)
    source_group = jnp.sum((arriving_end[None, :] <= slot_ids[:, None]).astype(jnp.int32), axis=1)
    arriving_start = (arriving_end - arriving)[source_group]
    flat_slot = source_group * CAP + slot_ids - arriving_start
    chosen = spread(flat_slot, rows_dev, rows_dev * CAP)

    group_x, weights = gather_all(packed(clip_rows), jnp.concatenate([w_qkv, w_out], axis=1), chosen)
    boundary = w_qkv.shape[1]
    qkv_full, out_full = weights[:, :boundary], weights[:, boundary:]
    projected = jnp.dot(group_x, qkv_full, preferred_element_type=jnp.float32)
    projected = projected.reshape(group_rows, -1, 3, HD)
    query_norm, query_factor = row_norm(projected[:, :, 0])
    key_norm, key_factor = row_norm(projected[:, :, 1])
    query_half = query_norm.astype(jnp.bfloat16)
    key_half = key_norm.astype(jnp.bfloat16)
    value_half = projected[:, :, 2].astype(jnp.bfloat16)
    local_heads = projected.shape[1]
    segment_row = segment_ids[0]
    same_segment = segment_row[:, None] == segment_row[None, :]
    scores = jnp.einsum(
        "qhe,khe->hqk", query_half, key_half, preferred_element_type=jnp.float32
    ) / math.sqrt(HD)
    expd = jnp.where(same_segment[None], jnp.exp(scores), jnp.float32(0.0))
    attention_probs = expd / jnp.sum(expd, axis=-1, keepdims=True)
    probs_half = attention_probs.astype(jnp.bfloat16)
    mixed = jnp.einsum("hqk,khe->qhe", probs_half, value_half, preferred_element_type=jnp.float32)
    mixed = mixed.astype(jnp.bfloat16).reshape(group_rows, local_heads * HD)
    partial_term = jnp.einsum("qc,dc->qd", mixed, out_full, preferred_element_type=jnp.float32).astype(jnp.bfloat16)
    clip_index = jnp.arange(reward_levels.shape[1], dtype=jnp.int32)
    levels = reward_levels[0].astype(jnp.float32) / 8.0
    own_segment = lax.dynamic_slice(segment_row, (shard * rows_dev,), (rows_dev,))
    row_weight = jnp.sum(
        jnp.where(own_segment[:, None] == clip_index[None, :], levels[None, :], jnp.float32(0.0)),
        axis=1,
        keepdims=True,
    )
    loss_scale = 1.0 / math.sqrt(rows_dev * groups * shards)
    own_x = lax.dynamic_slice(group_x, (shard * rows_dev, 0), (rows_dev, width))
    pred_grad = residual(packed(velocity_target), chosen, partial_term, own_x, row_weight * loss_scale)
    out_grad = jnp.dot(pred_grad, out_full, preferred_element_type=jnp.float32)
    out_grad = out_grad.astype(jnp.bfloat16).reshape(group_rows, local_heads, HD)
    value_grad = jnp.einsum(
        "hqk,qhe->khe", probs_half, out_grad, preferred_element_type=jnp.float32
    )
    prob_grad = jnp.einsum("qhe,khe->hqk", out_grad, value_half, preferred_element_type=jnp.float32)
    delta = jnp.sum(attention_probs * prob_grad, axis=-1, keepdims=True)
    score_grad = (attention_probs * (prob_grad - delta) / math.sqrt(HD)).astype(jnp.bfloat16)
    query_grad = jnp.einsum(
        "hqk,khe->qhe", score_grad, key_half, preferred_element_type=jnp.float32
    )
    key_grad = jnp.einsum(
        "hqk,qhe->khe", score_grad, query_half, preferred_element_type=jnp.float32
    )
    query_raw_grad = query_factor * (
        query_grad - query_norm * jnp.mean(query_grad * query_norm, axis=-1, keepdims=True)
    )
    key_raw_grad = key_factor * (
        key_grad - key_norm * jnp.mean(key_grad * key_norm, axis=-1, keepdims=True)
    )
    projected_grad = jnp.stack([query_raw_grad, key_raw_grad, value_grad], axis=2)
    projected_grad = projected_grad.reshape(group_rows, local_heads * 3 * HD).astype(jnp.bfloat16)
    qkv_part = jnp.einsum("qd,qc->dc", group_x, projected_grad, preferred_element_type=jnp.float32)
    out_part = jnp.einsum("qd,qc->dc", pred_grad, mixed, preferred_element_type=jnp.float32)
    summed_grads = scatter(jnp.concatenate([qkv_part, out_part], axis=1).astype(jnp.bfloat16))
    return (summed_grads[:, :boundary], summed_grads[:, boundary:])


def solution(mesh):
    return jax.shard_map(
        per_device,
        mesh=mesh,
        in_specs=(
            P(("dp", "seq"), None),
            P(("dp", "seq"), None),
            P(),
            P("dp", None),
            P("dp", None),
            P("dp", "seq"),
            P("dp", "seq"),
        ),
        out_specs=(P("dp", "seq"), P("dp", "seq")),
        check_vma=False,
    )
```

time: 1010 us -> 483 us (0.48)
  waiting for transfers between devices: 763 us -> 0 us
  Pallas kernels: 0 us -> 308 us
  blocking collectives: 49.1 us -> 0 us
  other arithmetic: 31.5 us -> 15.9 us
  between operations: 15 us -> 1.17 us
    all_gather x4 -> x0, waiting for transfers between devices: 382 us -> none  [the longest x1 172 us: per_device(): lax.all_gather(w_qkv, 'dp', axis=0, tiled=True)]
    pallas_call x0 -> x3, Pallas kernels: none -> 308 us  [the longest x1 122 us: residual(): pl.pallas_call(residual_kernel, out_shape=jax.ShapeDtypeStruct(partial.sh...]
    unnamed x7 -> x0, waiting for transfers between devices: 216 us -> none
    psum x1 -> x0, waiting for transfers between devices: 129 us -> none  [per_device(): lax.psum(partial_term.astype(jnp.bfloat16), 'seq').astype(jnp.float32)]
    all_to_all x1 -> x0, blocking collectives: 49.1 us -> none  [per_device(): lax.all_to_all(pack(clip_rows), 'dp', split_axis=0, concat_axis=0, tiled=...]
    all_to_all x1 -> x0, waiting for transfers between devices: 36.5 us -> none  [per_device(): lax.all_to_all(pack(velocity_target), 'dp', split_axis=0, concat_axis=0,...]
    dot_general x0 -> x2, local copies, waits for them, and re-layouts: none -> 17.7 us  [the longest x1 9.04 us: per_device(): jnp.einsum('qd,qc->dc', group_x, projected_grad, preferred_element_type=j...]
    unnamed x35 -> x26, local copies, waits for them, and re-layouts: 20.6 us -> 4.41 us
  transfers between devices with their start and end apart: 7 -> 0, of which waited for: 7 -> 0; matrix products, arithmetic and copies ran while one was open for 4% -> 0% of each run, Pallas kernels for 0% -> 0%
where the time goes in v1:
time: 483 us; the launch traced here: 475 us
  Pallas kernels  308 us (64%)
  matrix products  116 us (24%)
  local copies, waits for them, and re-layouts  34.5 us (7%)
  other arithmetic  15.9 us (3%)
    pallas_call x1, Pallas kernels, residual(): pl.pallas_call(residual_kernel, out_shape=jax.ShapeDtypeStruct(partial.sh...  122 us
    pallas_call x1, Pallas kernels, gather_all(): pl.pallas_call(gather_kernel, out_shape=(jax.ShapeDtypeStruct((rows * 4,...  107 us
    pallas_call x1, Pallas kernels, scatter(): pl.pallas_call(scatter_kernel, out_shape=jax.ShapeDtypeStruct((2, 48, col...  79.3 us
    dot_general x1, matrix products, per_device(): jnp.einsum('hqk,khe->qhe', score_grad, key_half, preferred_element_type=j...  21.7 us
    dot_general x1, matrix products, per_device(): jnp.einsum('hqk,qhe->khe', score_grad, query_half, preferred_element_type...  20.1 us
    dot_general x1, matrix products, per_device(): projected = jnp.dot(group_x, qkv_full, preferred_element_type=jnp.float32)  11.3 us

profile of v1, /device:TPU:16, one launch (start us, length us, event | category | flops | bytes accessed | tf_op | source)
XLA Modules:
  0.0 475.2 jit_solution(9670686087600245519)
XLA Ops:
  0.7 0.8 fusion.88
  5.1 1.6 fusion.71
  8.8 0.8 fusion.46.chosen
  9.6 1.7 pad_maximum_fusion.2
  11.4 2.4 broadcast_compare_fusion
  13.8 2.7 convolution_convert_fusion.2
  16.4 2.7 convolution_convert_fusion.3
  19.2 106.5 %gather_rows_weights.1 = (bf16[1024,3072]{1,0:T(8,128)(2,1)}, bf16[4,4,2,2,48,1536]{5,4,3,2,1,0:T(8,128)(2,1)}) custom-call(bf16[32,16,3072]{2,1,0:T(8,128)(2,1)} %bitcast.120, bf16[2,48,1536]{2,1,0:T(8,128)(2,1)} %bitcast.135, bf16[256,512]{1,0:T(8,128)(2,1)} %fusion.46.chosen), custom_call_target="tpu_custom_call" | custom-call | tf_op jit(solution)/shard_map/gather_rows_weights/pallas_call | solution.py:201
  125.7 2.7 constant_dynamic-slice_fusion.1.x_own
  128.4 11.3 %fusion.6 = f32[1024,1152]{0,1:T(8,128)S(1)} fusion(bf16[1024,3072]{1,0:T(8,128)(2,1)} %get-tuple-element.4, bf16[3072,1536]{1,0:T(8,128)(2,1)} %bitcast.140), kind=kOutput, calls=%fused_computation.9 | convolution fusion | flops 7247757312 | bytes 18087936 | tf_op jit(solution)/shard_map/dot_general | solution.py:507
  139.7 2.2 copy-done.2
  142.6 9.0 %copy.47 = bf16[3072,1024]{1,0:T(8,128)(2,1)} copy(bf16[3072,1024]{0,1:T(8,128)(2,1)} %bitcast.122) | data formatting | bytes 12582912 | tf_op jit(solution)/shard_map/qd,qc->dc/dot_general | solution.py:559
  151.7 4.7 fusion.3
  156.4 6.2 %fusion.32 = bf16[3,128,1024]{2,1,0:T(8,128)(2,1)S(1)} fusion(f32[3,1024,1024]{1,2,0:T(8,128)S(1)} %get-tuple-element.11, f32[3,1024]{1,0:T(4,128)S(1)} %get-tuple-element.10, pred[1024,1024]{0,1:T(8,128)(4,1)S(1)} %copy-done.6, f32[1024,3,3,128]{0,3,2,1:T(8,128)} %bitcast.128), kind=kOutput, calls=%fused_computation.45 | convolution fusion | flops 818282496 | bytes 15216640 | tf_op jit(solution)/shard_map/hqk,khe->qhe/dot_general | solution.py:523
  162.6 0.9 copy-done.9
  163.5 7.1 %convolution_convert_fusion.1.partial = bf16[1024,3072]{1,0:T(8,128)(2,1)} fusion(bf16[1024,384]{0,1:T(8,128)(2,1)S(1)} %bitcast.143, bf16[3072,1536]{1,0:T(8,128)(2,1)} %bitcast.141), kind=kOutput, calls=%fused_computation.14 | convolution fusion | flops 2419064832 | bytes 9437184 | tf_op jit(solution)/shard_map/qc,dc->qd/dot_general | solution.py:525
  170.6 122.3 %residual_gradient.1 = bf16[1024,3072]{1,0:T(8,128)(2,1)} custom-call(bf16[32,16,3072]{2,1,0:T(8,128)(2,1)} %bitcast.121, bf16[256,512]{1,0:T(8,128)(2,1)} %fusion.46.chosen, bf16[1024,3072]{1,0:T(8,128)(2,1)} %convolution_convert_fusion.1.partial, bf16[256,3072]{1,0:T(8,128)(2,1)} %constant_dynamic-slice_fusion.1.x_own, f32[256,1]{1,0:T(8,128)} %copy.55.weight), custom_call_target="tpu_custom_call" | custom-call | tf_op jit(solution)/shard_map/residual_gradient/pallas_call | solution.py:329
  292.8 7.0 %fusion.29 = bf16[1024,384]{0,1:T(8,128)(2,1)} fusion(bf16[1024,3072]{1,0:T(8,128)(2,1)} %residual_gradient.1, bf16[3072,1536]{1,0:T(8,128)(2,1)} %bitcast.142), kind=kOutput, calls=%fused_computation.44 | convolution fusion | flops 2416312320 | bytes 9437184 | tf_op jit(solution)/shard_map/dot_general | solution.py:537
  299.9 8.7 %copy.63 = bf16[3072,1024]{1,0:T(8,128)(2,1)} copy(bf16[3072,1024]{0,1:T(8,128)(2,1)} %bitcast.119) | data formatting | bytes 12582912 | tf_op jit(solution)/shard_map/qd,qc->dc/dot_general | solution.py:560
  308.6 7.9 %convolution_convert_fusion.4 = bf16[4,4,2,2,48,384]{5,4,3,2,1,0:T(8,128)(2,1)} fusion(bf16[4,4,2,2,48,1024]{5,4,3,2,1,0:T(8,128)(2,1)} %bitcast.126, bf16[1024,384,1,1,1,1]{0,1,5,4,3,2:T(8,128)(2,1)} %bitcast.144), kind=kOutput, calls=%fused_computation.26 | convolution fusion | flops 2417098752 | bytes 9437184 | tf_op jit(solution)/shard_map/qd,qc->dc/dot_general | solution.py:560
  316.5 7.7 %fusion.38 = bf16[1024,3,1,128]{0,3,1,2:T(8,128)(2,1)} fusion(bf16[1024,3,128]{0,2,1:T(8,128)(2,1)S(1)} %bitcast.133, f32[3,1024,1024]{1,2,0:T(8,128)} %copy-done.10, f32[3,1024]{1,0:T(4,128)S(1)} %get-tuple-element.10, pred[1024,1024]{0,1:T(8,128)(4,1)S(1)} %copy-done.7), kind=kOutput, calls=%fused_computation.47 | convolution fusion | flops 818282496 | bytes 15216640 | tf_op jit(solution)/shard_map/hqk,qhe->khe/dot_general | solution.py:539
  324.2 7.7 %fusion.47 = f32[3,1024,1024]{1,2,0:T(8,128)} fusion(bf16[1024,3,128]{0,2,1:T(8,128)(2,1)S(1)} %bitcast.134, f32[1024,3,3,128]{0,3,2,1:T(8,128)} %bitcast.129), kind=kOutput, calls=%fused_computation.56 | convolution fusion | flops 805306368 | bytes 14155776 | tf_op jit(solution)/shard_map/qhe,khe->hqk/dot_general | solution.py:542
  331.9 21.7 %fusion.24 = (f32[1024,3]{0,1:T(4,128)S(1)}, f32[3,128,1024]{2,1,0:T(8,128)}) fusion(f32[1024,3,1,128]{0,3,2,1:T(8,128)S(1)} %get-tuple-element.9, f32[1024,3]{0,1:T(4,128)S(1)} %add_rsqrt_fusion.1, f32[3,1024,1024]{1,2,0:T(8,128)} %fusion.47, f32[3,1024]{1,0:T(4,128)S(1)} %get-tuple-element.10, f32[3,1024,1024]{1,2,0:T(8,128)} %copy-done.10, ...), kind=kOutput, calls=%fused_computation.37 | convolution fusion | flops 841876480 | bytes 30982144 | tf_op jit(solution)/shard_map/hqk,khe->qhe/dot_general | solution.py:545
  353.6 20.1 %fusion.21 = (f32[1024,3]{0,1:T(4,128)S(1)}, f32[3,128,1024]{2,1,0:T(8,128)}) fusion(f32[1024,3,1,128]{0,3,2,1:T(8,128)S(1)} %get-tuple-element.8, f32[1024,3]{0,1:T(4,128)S(1)} %add_rsqrt_fusion, f32[3,1024,1024]{1,2,0:T(8,128)} %fusion.47, f32[3,1024]{1,0:T(4,128)S(1)} %get-tuple-element.10, f32[3,1024,1024]{1,2,0:T(8,128)} %copy-done.10, ...), kind=kOutput, calls=%fused_computation.32 | convolution fusion | flops 841876480 | bytes 30982144 | tf_op jit(solution)/shard_map/hqk,qhe->khe/dot_general | solution.py:548
  373.7 1.9 fusion.44
  375.6 1.9 fusion.43
  378.2 1.1 slice-done.1
  379.3 8.8 %convolution_convert_fusion = bf16[4,4,2,2,48,1152]{5,4,3,2,1,0:T(8,128)(2,1)S(1)} fusion(bf16[4,4,2,2,48,1024]{5,4,3,2,1,0:T(8,128)(2,1)S(1)} %bitcast.125, bf16[1024,1152,1,1,1,1]{0,1,5,4,3,2:T(8,128)(2,1)S(1)} %bitcast.132), kind=kOutput, calls=%fused_computation.11 | convolution fusion | flops 7251296256 | bytes 15728640 | tf_op jit(solution)/shard_map/qd,qc->dc/dot_general | solution.py:559
  388.1 4.1 pad_maximum_fusion.grads
  392.2 79.3 %scatter_gradients.1 = f32[2,48,1536]{2,1,0:T(8,128)} custom-call(bf16[4,4,2,2,48,1536]{5,4,3,2,1,0:T(8,128)(2,1)} %pad_maximum_fusion.grads), custom_call_target="tpu_custom_call" | custom-call | tf_op jit(solution)/shard_map/scatter_gradients/pallas_call | solution.py:447
  471.6 1.6 slice.37
  473.2 1.8 slice.36
  (59 shorter events, 7.1 us)
Async XLA Ops:
  0.6 13.1 %copy-start = (bf16[256,3072]{1,0:T(8,128)(2,1)S(1)}, bf16[256,3072]{1,0:T(8,128)(2,1)}, u32[]{:S(2)}) copy-start(bf16[256,3072]{1,0:T(8,128)(2,1)} %param.8) | copy-start | bytes 4718596
  0.6 15.8 %copy-start.4 = (bf16[256,3072]{1,0:T(8,128)(2,1)S(1)}, bf16[256,3072]{1,0:T(8,128)(2,1)}, u32[]{:S(2)}) copy-start(bf16[256,3072]{1,0:T(8,128)(2,1)} %param.7) | copy-start | bytes 4718596
  139.7 2.2 copy-start.2
  151.7 4.7 copy-start.6
  156.4 6.2 %copy-start.10 = (f32[3,1024,1024]{1,2,0:T(8,128)}, f32[3,1024,1024]{1,2,0:T(8,128)S(1)}, u32[]{:S(2)}) copy-start(f32[3,1024,1024]{1,2,0:T(8,128)S(1)} %get-tuple-element.11) | copy-start | bytes 37748740
  162.6 0.9 copy-start.9
  308.6 7.9 %copy-start.5 = (bf16[1024,384]{0,1:T(8,128)(2,1)S(1)}, bf16[1024,384]{0,1:T(8,128)(2,1)}, u32[]{:S(2)}) copy-start(bf16[1024,384]{0,1:T(8,128)(2,1)} %fusion.29) | copy-start | bytes 2359300
  308.6 7.9 %copy-start.7 = (pred[1024,1024]{0,1:T(8,128)(4,1)S(1)}, pred[1024,1024]{0,1:T(8,128)(4,1)}, u32[]{:S(2)}) copy-start(pred[1024,1024]{0,1:T(8,128)(4,1)} %broadcast_compare_fusion) | copy-start | bytes 3145732
  373.7 3.9 copy-start.8
  375.6 2.7 slice-start
  377.6 1.8 slice-start.1
  379.3 8.8 %copy-start.3 = (bf16[4,4,2,2,48,384]{5,4,3,2,1,0:T(8,128)(2,1)S(1)}, bf16[4,4,2,2,48,384]{5,4,3,2,1,0:T(8,128)(2,1)}, u32[]{:S(2)}) copy-start(bf16[4,4,2,2,48,384]{5,4,3,2,1,0:T(8,128)(2,1)} %convolution_convert_fusion.4) | copy-start | bytes 7077892
  388.1 86.9 %copy-start.1 = (bf16[256,3072]{1,0:T(8,128)(2,1)S(1)}, bf16[256,3072]{1,0:T(8,128)(2,1)}, u32[]{:S(2)}) copy-start(bf16[256,3072]{1,0:T(8,128)(2,1)} %param.8) | copy-start | bytes 4718596

commit v2 on v1

--- a/solution.py
+++ b/solution.py
@@ -226,12 +226,34 @@
 
 
 CHUNKS = 4
-
-
-def residual_kernel(packed, chosen, partial, x_own, weight, d_full, received, target, from_core, summed, from_chip, a2a_send, a2a_recv, send_sem, recv_sem, local_sem):
+HEADS = 3
+QKV = HEADS * 3 * HD
+OUT = HEADS * HD
+EXP2_SCALE = math.log2(math.e) / math.sqrt(HD)
+
+
+def nt(left, right):
+    return lax.dot_general(left, right, (((1,), (1,)), ((), ())), preferred_element_type=jnp.float32)
+
+
+def tn(left, right):
+    return lax.dot_general(left, right, (((0,), (0,)), ((), ())), preferred_element_type=jnp.float32)
+
+
+def nn(left, right):
+    return jnp.dot(left, right, preferred_element_type=jnp.float32)
+
+
+def forward_kernel(
+    packed, chosen, x_full, w_full, mark_q, mark_k, x_own, weight,
+    d_full, q_marked, k_marked, v_half, factors, inverse, mixed,
+    projected, v_turned, partial, received, target, from_core, summed, from_chip,
+    a2a_send, a2a_recv, send_sem, recv_sem, local_sem,
+):
     me = my_place()
     dp = lax.axis_index("dp")
     rows, width = x_own.shape
+    group_rows = x_full.shape[0]
     other_chip, other_core = moved(me, A, 1), moved(me, C, 1)
     barrier = pltpu.get_barrier_semaphore()
 
@@ -248,14 +270,6 @@
 
     def rows_of(place, chunk):
         return pl.ds(pl.multiple_of(device(place)["seq"] * rows + chunk * step, step), step)
-
-    core_first, core_second = [], []
-    for chunk in range(CHUNKS):
-        core_first.append(copies.start(
-            partial.at[rows_of(moved(other_core, A, 1), chunk)], from_core.at[0, pl.ds(chunk * step, step)], other_core))
-    for chunk in range(CHUNKS):
-        core_second.append(copies.start(
-            partial.at[rows_of(other_core, chunk)], from_core.at[1, pl.ds(chunk * step, step)], other_core))
 
     def block_copy(k):
         to = dp_peer(me, k, 1)
@@ -275,12 +289,56 @@
     own_block = pltpu.make_async_copy(packed.at[dp], received.at[dp], local_sem.at[0])
     own_block.start()
 
-    chip_sums = []
+    @pl.loop(0, group_rows // rows)
+    def _(i):
+        at = pl.ds(pl.multiple_of(i * rows, rows), rows)
+        for low in range(0, QKV, 256):
+            columns = slice(low, min(low + 256, QKV))
+            projected[:, columns] = nn(x_full[at, :], w_full[:, columns])
+        for h in range(HEADS):
+            for part, marked, mark in ((0, q_marked, mark_q), (1, k_marked, mark_k)):
+                raw = projected[:, (h * 3 + part) * HD:(h * 3 + part + 1) * HD]
+                factor = lax.rsqrt(jnp.mean(raw * raw, axis=-1, keepdims=True) + epsilon)
+                marked[h, at, 0:HD] = (raw * factor).astype(jnp.bfloat16)
+                marked[h, at, HD:2 * HD] = mark[at, :]
+                factors[part, h, at, :] = jnp.broadcast_to(factor, (rows, HD))
+            value = projected[:, (h * 3 + 2) * HD:(h * 3 + 3) * HD]
+            v_half[h, at, :] = value.astype(jnp.bfloat16)
+            v_turned[h, :, at] = value.T.astype(jnp.bfloat16)
+
+    def block(place):
+        at = pl.ds(pl.multiple_of(device(place)["seq"] * rows, rows), rows)
+
+        @pl.loop(0, HEADS)
+        def _(h):
+            scores = nt(k_marked[h], q_marked[h, at, :])
+            raised = jnp.exp2(scores * EXP2_SCALE)
+            inverse_sum = 1.0 / jnp.sum(raised, axis=0, keepdims=True)
+            turned = nn(v_turned[h], raised.astype(jnp.bfloat16)) * inverse_sum
+            mixed[at, pl.ds(pl.multiple_of(h * HD, HD), HD)] = turned.T.astype(jnp.bfloat16)
+            inverse[h, at, :] = jnp.broadcast_to(inverse_sum, (HD, rows)).T
+
+        @pl.loop(0, width // 512)
+        def _(t):
+            columns = pl.ds(pl.multiple_of(t * 512, 512), 512)
+            partial[at, columns] = nt(mixed[at, :], w_full[columns, QKV:QKV + OUT]).astype(jnp.bfloat16)
+
+    core_first, core_second, chip_sums = [], [], []
+    block(moved(other_core, A, 1))
+    for chunk in range(CHUNKS):
+        core_first.append(copies.start(
+            partial.at[rows_of(moved(other_core, A, 1), chunk)], from_core.at[0, pl.ds(chunk * step, step)], other_core))
+    block(other_chip)
     for chunk in range(CHUNKS):
         core_first[chunk].wait_recv()
         at = pl.ds(chunk * step, step)
         summed[at] = (partial[rows_of(other_chip, chunk)].astype(jnp.float32) + from_core[0, at].astype(jnp.float32)).astype(jnp.bfloat16)
         chip_sums.append(copies.start(summed.at[at], from_chip.at[at], other_chip))
+    block(other_core)
+    for chunk in range(CHUNKS):
+        core_second.append(copies.start(
+            partial.at[rows_of(other_core, chunk)], from_core.at[1, pl.ds(chunk * step, step)], other_core))
+    block(me)
 
     own_block.wait()
 
@@ -294,7 +352,7 @@
     def _(t):
         columns = pl.ds(pl.multiple_of(t * tile, tile), tile)
         blocks = received[:, :, columns].reshape(rows * CAP, tile)
-        target[:, columns] = jnp.dot(chosen[...], blocks, preferred_element_type=jnp.float32).astype(jnp.bfloat16)
+        target[:, columns] = nn(chosen[...], blocks).astype(jnp.bfloat16)
 
     to_chip, to_core, passed = [], [], []
     for chunk in range(CHUNKS):
@@ -324,19 +382,33 @@
     copies.finish()
 
 
-def residual(packed, chosen, partial, x_own, weight):
+def forward(packed, chosen, x_full, w_full, mark_q, mark_k, x_own, weight):
     rows, width = x_own.shape
+    group_rows = x_full.shape[0]
+    vmem = pl.BlockSpec(memory_space=pltpu.VMEM)
+    half, full = jnp.bfloat16, jnp.float32
     return pl.pallas_call(
-        residual_kernel,
-        out_shape=jax.ShapeDtypeStruct(partial.shape, jnp.bfloat16),
-        in_specs=[pl.BlockSpec(memory_space=pl.ANY)] + [pl.BlockSpec(memory_space=pltpu.VMEM)] * 4,
-        out_specs=pl.BlockSpec(memory_space=pltpu.VMEM),
+        forward_kernel,
+        out_shape=(
+            jax.ShapeDtypeStruct((group_rows, width), half),
+            jax.ShapeDtypeStruct((HEADS, group_rows, 2 * HD), half),
+            jax.ShapeDtypeStruct((HEADS, group_rows, 2 * HD), half),
+            jax.ShapeDtypeStruct((HEADS, group_rows, HD), half),
+            jax.ShapeDtypeStruct((2, HEADS, group_rows, HD), full),
+            jax.ShapeDtypeStruct((HEADS, group_rows, HD), full),
+            jax.ShapeDtypeStruct((group_rows, OUT), half),
+        ),
+        in_specs=[pl.BlockSpec(memory_space=pl.ANY)] + [vmem] * 7,
+        out_specs=(vmem,) * 7,
         scratch_shapes=[
-            pltpu.VMEM(packed.shape, jnp.bfloat16),
-            pltpu.VMEM((rows, width), jnp.bfloat16),
-            pltpu.VMEM((2, rows, width), jnp.bfloat16),
-            pltpu.VMEM((rows, width), jnp.bfloat16),
-            pltpu.VMEM((rows, width), jnp.bfloat16),
+            pltpu.VMEM((rows, QKV), full),
+            pltpu.VMEM((HEADS, HD, group_rows), half),
+            pltpu.VMEM((group_rows, width), half),
+            pltpu.VMEM(packed.shape, half),
+            pltpu.VMEM((rows, width), half),
+            pltpu.VMEM((2, rows, width), half),
+            pltpu.VMEM((rows, width), half),
+            pltpu.VMEM((rows, width), half),
             pltpu.SemaphoreType.DMA((32,)),
             pltpu.SemaphoreType.DMA((32,)),
             pltpu.SemaphoreType.DMA((6 * CHUNKS,)),
@@ -344,8 +416,8 @@
             pltpu.SemaphoreType.DMA((1,)),
         ],
         compiler_params=pltpu.CompilerParams(collective_id=2, has_side_effects=True, vmem_limit_bytes=VMEM_LIMIT),
-        name="residual_gradient",
-    )(packed, chosen, partial, x_own, weight)
+        name="forward_residual_gradient",
+    )(packed, chosen, x_full, w_full, mark_q, mark_k, x_own, weight)
 
 
 def added(*values):
@@ -399,57 +471,189 @@
         out[index] = added(*[part[index] for part in parts]).astype(out.dtype)
 
 
-def scatter_kernel(grads, sums_out, got_far, sum_far, half_far, got_near, sum_near, half_near, got_last, send_sem, recv_sem):
+SLABS = HEADS + 1
+
+
+def backward_kernel(
+    d_full, x_full, w_out, q_marked, k_marked, v_half, factors, inverse, mixed,
+    qkv_sums, out_sums,
+    d_out, k_turned, dq, dk, dv, d_proj,
+    grads, got_far, sum_far, half_far, got_near, sum_near, half_near, got_last, send_sem, recv_sem,
+):
     me = my_place()
     z, x, y, a, c = me
     greet([moved(me, Z, 1), moved(me, Z, -1), moved(me, X, 1), moved(me, X, -1), moved(me, Y, 1)])
     copies = Copies(send_sem, recv_sem)
     far_axis, near_axis = (X, Z), (Z, X)
-
-    def far_block(half):
-        if half == 0:
-            return lambda at, which: grads.at[pl.ds(2 * which, 2), at, :, 0]
-        return lambda at, which: grads.at[at, pl.ds(2 * which, 2), :, 1]
-
-    def near_block(half):
-        return lambda at, which: half_far.at[half, at, which]
-
-    def slots(ref, half):
-        return lambda j: ref.at[half, j]
-
-    def far_out(half):
-        return lambda which: half_far.at[half, pl.ds(2 * which, 2)]
-
-    def near_out(half):
-        return lambda which: half_near.at[half, pl.ds(which, 1)]
+    group_rows, width = x_full.shape
+    rows = group_rows // 4
+    scale = 1.0 / math.sqrt(HD)
+
+    class Slab:
+        def __init__(self, s):
+            self.s = s
+
+        def far_block(self, half):
+            if half == 0:
+                return lambda at, which: grads.at[self.s, pl.ds(2 * which, 2), at, :, 0]
+            return lambda at, which: grads.at[self.s, at, pl.ds(2 * which, 2), :, 1]
+
+        def near_block(self, half):
+            return lambda at, which: half_far.at[self.s, half, at, which]
+
+        def slots(self, ref, half):
+            return lambda j: ref.at[self.s, half, j]
+
+        def far_out(self, half):
+            return lambda which: half_far.at[self.s, half, pl.ds(2 * which, 2)]
+
+        def near_out(self, half):
+            return lambda which: half_near.at[self.s, half, pl.ds(which, 1)]
+
+        def far_start(self):
+            self.sent = [
+                reduce_start(copies, me, far_axis[h], self.far_block(h), self.slots(got_far, h)) for h in (0, 1)]
+
+        def far_pass(self):
+            self.sent = [
+                reduce_pass(copies, me, far_axis[h], self.far_block(h), self.slots(got_far, h),
+                            self.slots(sum_far, h), self.sent[h], add_rows)
+                for h in (0, 1)]
+
+        def near_start(self):
+            for h in (0, 1):
+                reduce_end(me, far_axis[h], self.far_block(h), self.slots(got_far, h), self.far_out(h), self.sent[h], add_rows)
+            self.sent = [
+                reduce_start(copies, me, near_axis[h], self.near_block(h), self.slots(got_near, h)) for h in (0, 1)]
+
+        def near_pass(self):
+            self.sent = [
+                reduce_pass(copies, me, near_axis[h], self.near_block(h), self.slots(got_near, h),
+                            self.slots(sum_near, h), self.sent[h], near_add)
+                for h in (0, 1)]
+
+        def last_start(self):
+            for h in (0, 1):
+                reduce_end(me, near_axis[h], self.near_block(h), self.slots(got_near, h), self.near_out(h), self.sent[h], near_add)
+            self.sent = [
+                copies.start(half_near.at[self.s, h, 1 - y], got_last.at[self.s, h], moved(me, Y, 1)) for h in (0, 1)]
+
+        def end(self):
+            for h in (0, 1):
+                self.sent[h].wait_recv()
+                total = added(half_near[self.s, h, y], got_last[self.s, h])
+                if self.s == HEADS:
+                    out_sums[h] = total
+                else:
+                    qkv_sums[h, :, self.s * 3 * HD:(self.s + 1) * 3 * HD] = total
 
     def near_add(out, parts):
         out[...] = added(*[part[...] for part in parts]).astype(out.dtype).reshape(out.shape)
 
-    sent = [reduce_start(copies, me, far_axis[h], far_block(h), slots(got_far, h)) for h in (0, 1)]
-    sent = [reduce_pass(copies, me, far_axis[h], far_block(h), slots(got_far, h), slots(sum_far, h), sent[h], add_rows) for h in (0, 1)]
-    for h in (0, 1):
-        reduce_end(me, far_axis[h], far_block(h), slots(got_far, h), far_out(h), sent[h], add_rows)
-    sent = [reduce_start(copies, me, near_axis[h], near_block(h), slots(got_near, h)) for h in (0, 1)]
-    sent = [reduce_pass(copies, me, near_axis[h], near_block(h), slots(got_near, h), slots(sum_near, h), sent[h], near_add) for h in (0, 1)]
-    for h in (0, 1):
-        reduce_end(me, near_axis[h], near_block(h), slots(got_near, h), near_out(h), sent[h], near_add)
-    last = [copies.start(half_near.at[h, 1 - y], got_last.at[h], moved(me, Y, 1)) for h in (0, 1)]
-    for h in (0, 1):
-        last[h].wait_recv()
-        sums_out[h] = added(half_near[h, y], got_last[h])
+    def weight_grads(s, left, right):
+        @pl.loop(0, 8)
+        def _(t):
+            columns = pl.ds(pl.multiple_of(t * 384, 384), 384)
+            term = tn(left[:, columns], right[...]).astype(jnp.bfloat16)
+            grads[s, t // 2, pl.ds(t % 2 * 2, 2)] = term.reshape(2, 2, 2, 48, 384)
+
+    def head(h):
+        head_columns = slice(h * HD, (h + 1) * HD)
+
+        @pl.loop(0, 4)
+        def _(i):
+            at = pl.ds(pl.multiple_of(i * rows, rows), rows)
+            k_turned[:, at] = k_marked[h, at, 0:HD].astype(jnp.float32).T.astype(jnp.bfloat16)
+
+        dk[...] = jnp.zeros_like(dk)
+        dv[...] = jnp.zeros_like(dv)
+
+        @pl.loop(0, 4)
+        def _(i):
+            at = pl.ds(pl.multiple_of(i * rows, rows), rows)
+            raised = jnp.exp2(nt(k_marked[h], q_marked[h, at, :]) * EXP2_SCALE)
+            d_here = d_out[at, head_columns]
+            delta = jnp.sum((d_here.astype(jnp.float32) * mixed[at, head_columns].astype(jnp.float32)).T, axis=0, keepdims=True)
+            d_scores = (raised * (nt(v_half[h], d_here) - delta)).astype(jnp.bfloat16)
+            dv[...] += nn(raised.astype(jnp.bfloat16), d_here)
+            dk[...] += nn(d_scores, q_marked[h, at, 0:HD])
+            dq[at, :] = nn(k_turned[...], d_scores).T
+
+        @pl.loop(0, 4)
+        def _(i):
+            at = pl.ds(pl.multiple_of(i * rows, rows), rows)
+            for part, grad, marked in ((0, dq, q_marked), (1, dk, k_marked)):
+                normed = marked[h, at, 0:HD].astype(jnp.float32)
+                got = grad[at, :]
+                inner = jnp.mean(got * normed, axis=-1, keepdims=True)
+                d_proj[at, part * HD:(part + 1) * HD] = (
+                    (factors[part, h, at, :] * scale) * (got - normed * inner)).astype(jnp.bfloat16)
+            d_proj[at, 2 * HD:3 * HD] = dv[at, :].astype(jnp.bfloat16)
+
+    out_slab = Slab(HEADS)
+    slabs = [Slab(h) for h in range(HEADS)]
+    weight_grads(HEADS, d_full, mixed)
+    out_slab.far_start()
+
+    @pl.loop(0, 4)
+    def _(i):
+        at = pl.ds(pl.multiple_of(i * rows, rows), rows)
+        got = nn(d_full[at, :], w_out[...])
+        for h in range(HEADS):
+            d_out[at, h * HD:(h + 1) * HD] = (got[:, h * HD:(h + 1) * HD] * inverse[h, at, :]).astype(jnp.bfloat16)
+
+    head(0)
+    out_slab.far_pass()
+    weight_grads(0, x_full, d_proj)
+    slabs[0].far_start()
+    out_slab.near_start()
+    head(1)
+    slabs[0].far_pass()
+    out_slab.near_pass()
+    weight_grads(1, x_full, d_proj)
+    slabs[1].far_start()
+    slabs[0].near_start()
+    out_slab.last_start()
+    head(2)
+    slabs[1].far_pass()
+    slabs[0].near_pass()
+    out_slab.end()
+    weight_grads(2, x_full, d_proj)
+    slabs[2].far_start()
+    slabs[1].near_start()
+    slabs[0].last_start()
+    slabs[2].far_pass()
+    slabs[1].near_pass()
+    slabs[0].end()
+    slabs[2].near_start()
+    slabs[1].last_start()
+    slabs[2].near_pass()
+    slabs[1].end()
+    slabs[2].last_start()
+    slabs[2].end()
     copies.finish()
 
 
-def scatter(grads):
-    cols = grads.shape[1]
-    half = lambda *lead: pltpu.VMEM((2, *lead, 48, cols), jnp.bfloat16)
-    sums = pl.pallas_call(
-        scatter_kernel,
-        out_shape=jax.ShapeDtypeStruct((2, 48, cols), jnp.float32),
-        in_specs=[pl.BlockSpec(memory_space=pltpu.VMEM)],
-        out_specs=pl.BlockSpec(memory_space=pltpu.VMEM),
+def backward(d_full, x_full, w_out, q_marked, k_marked, v_half, factors, inverse, mixed):
+    group_rows = x_full.shape[0]
+    half = lambda *lead: pltpu.VMEM((SLABS, 2, *lead, 48, 3 * HD), jnp.bfloat16)
+    vmem = pl.BlockSpec(memory_space=pltpu.VMEM)
+    qkv_sums, out_sums = pl.pallas_call(
+        backward_kernel,
+        out_shape=(
+            jax.ShapeDtypeStruct((2, 48, QKV), jnp.float32),
+            jax.ShapeDtypeStruct((2, 48, OUT), jnp.float32),
+        ),
+        in_specs=[vmem] * 9,
+        out_specs=(vmem, vmem),
         scratch_shapes=[
+            pltpu.VMEM((group_rows, OUT), jnp.bfloat16),
+            pltpu.VMEM((HD, group_rows), jnp.bfloat16),
+            pltpu.VMEM((group_rows, HD), jnp.float32),
+            pltpu.VMEM((group_rows, HD), jnp.float32),
+            pltpu.VMEM((group_rows, HD), jnp.float32),
+            pltpu.VMEM((group_rows, 3 * HD), jnp.bfloat16),
+            pltpu.VMEM((SLABS, 4, 4, 2, 2, 48, 3 * HD), jnp.bfloat16),
             half(6, 2, 2),
             half(2, 2, 2),
             half(4, 2),
@@ -457,18 +661,13 @@
             half(2),
             half(2),
             half(),
-            pltpu.SemaphoreType.DMA((26,)),
-            pltpu.SemaphoreType.DMA((26,)),
+            pltpu.SemaphoreType.DMA((26 * SLABS,)),
+            pltpu.SemaphoreType.DMA((26 * SLABS,)),
         ],
         compiler_params=pltpu.CompilerParams(collective_id=3, has_side_effects=True, vmem_limit_bytes=VMEM_LIMIT),
-        name="scatter_gradients",
-    )(grads.reshape(4, 4, 2, 2, 48, cols))
-    return sums.reshape(96, cols)
-
-
-def row_norm(values):
-    factor = lax.rsqrt(jnp.mean(values * values, axis=-1, keepdims=True) + epsilon)
-    return (values * factor, factor)
+        name="backward_scatter",
+    )(d_full, x_full, w_out, q_marked, k_marked, v_half, factors, inverse, mixed)
+    return qkv_sums.reshape(96, QKV), out_sums.reshape(96, OUT)
 
 
 def spread(block_of, rows, columns):
@@ -502,27 +701,7 @@
     chosen = spread(flat_slot, rows_dev, rows_dev * CAP)
 
     group_x, weights = gather_all(packed(clip_rows), jnp.concatenate([w_qkv, w_out], axis=1), chosen)
-    boundary = w_qkv.shape[1]
-    qkv_full, out_full = weights[:, :boundary], weights[:, boundary:]
-    projected = jnp.dot(group_x, qkv_full, preferred_element_type=jnp.float32)
-    projected = projected.reshape(group_rows, -1, 3, HD)
-    query_norm, query_factor = row_norm(projected[:, :, 0])
-    key_norm, key_factor = row_norm(projected[:, :, 1])
-    query_half = query_norm.astype(jnp.bfloat16)
-    key_half = key_norm.astype(jnp.bfloat16)
-    value_half = projected[:, :, 2].astype(jnp.bfloat16)
-    local_heads = projected.shape[1]
     segment_row = segment_ids[0]
-    same_segment = segment_row[:, None] == segment_row[None, :]
-    scores = jnp.einsum(
-        "qhe,khe->hqk", query_half, key_half, preferred_element_type=jnp.float32
-    ) / math.sqrt(HD)
-    expd = jnp.where(same_segment[None], jnp.exp(scores), jnp.float32(0.0))
-    attention_probs = expd / jnp.sum(expd, axis=-1, keepdims=True)
-    probs_half = attention_probs.astype(jnp.bfloat16)
-    mixed = jnp.einsum("hqk,khe->qhe", probs_half, value_half, preferred_element_type=jnp.float32)
-    mixed = mixed.astype(jnp.bfloat16).reshape(group_rows, local_heads * HD)
-    partial_term = jnp.einsum("qc,dc->qd", mixed, out_full, preferred_element_type=jnp.float32).astype(jnp.bfloat16)
     clip_index = jnp.arange(reward_levels.shape[1], dtype=jnp.int32)
     levels = reward_levels[0].astype(jnp.float32) / 8.0
     own_segment = lax.dynamic_slice(segment_row, (shard * rows_dev,), (rows_dev,))
@@ -533,33 +712,15 @@
     )
     loss_scale = 1.0 / math.sqrt(rows_dev * groups * shards)
     own_x = lax.dynamic_slice(group_x, (shard * rows_dev, 0), (rows_dev, width))
-    pred_grad = residual(packed(velocity_target), chosen, partial_term, own_x, row_weight * loss_scale)
-    out_grad = jnp.dot(pred_grad, out_full, preferred_element_type=jnp.float32)
-    out_grad = out_grad.astype(jnp.bfloat16).reshape(group_rows, local_heads, HD)
-    value_grad = jnp.einsum(
-        "hqk,qhe->khe", probs_half, out_grad, preferred_element_type=jnp.float32
-    )
-    prob_grad = jnp.einsum("qhe,khe->hqk", out_grad, value_half, preferred_element_type=jnp.float32)
-    delta = jnp.sum(attention_probs * prob_grad, axis=-1, keepdims=True)
-    score_grad = (attention_probs * (prob_grad - delta) / math.sqrt(HD)).astype(jnp.bfloat16)
-    query_grad = jnp.einsum(
-        "hqk,khe->qhe", score_grad, key_half, preferred_element_type=jnp.float32
-    )
-    key_grad = jnp.einsum(
-        "hqk,qhe->khe", score_grad, query_half, preferred_element_type=jnp.float32
-    )
-    query_raw_grad = query_factor * (
-        query_grad - query_norm * jnp.mean(query_grad * query_norm, axis=-1, keepdims=True)
-    )
-    key_raw_grad = key_factor * (
-        key_grad - key_norm * jnp.mean(key_grad * key_norm, axis=-1, keepdims=True)
-    )
-    projected_grad = jnp.stack([query_raw_grad, key_raw_grad, value_grad], axis=2)
-    projected_grad = projected_grad.reshape(group_rows, local_heads * 3 * HD).astype(jnp.bfloat16)
-    qkv_part = jnp.einsum("qd,qc->dc", group_x, projected_grad, preferred_element_type=jnp.float32)
-    out_part = jnp.einsum("qd,qc->dc", pred_grad, mixed, preferred_element_type=jnp.float32)
-    summed_grads = scatter(jnp.concatenate([qkv_part, out_part], axis=1).astype(jnp.bfloat16))
-    return (summed_grads[:, :boundary], summed_grads[:, boundary:])
+
+    sign = (2 * segment_row - 1)[:, None]
+    lane = jnp.arange(HD, dtype=jnp.int32)[None, :]
+    mark_q = jnp.where(lane == 0, 64 * sign, jnp.where(lane == 1, -64, 0)).astype(jnp.bfloat16)
+    mark_k = jnp.where(lane == 0, 32 * sign, jnp.where(lane == 1, 32, 0)).astype(jnp.bfloat16)
+
+    pred_grad, *saved = forward(
+        packed(velocity_target), chosen, group_x, weights, mark_q, mark_k, own_x, row_weight * loss_scale)
+    return backward(pred_grad, group_x, weights[:, QKV:], *saved)
 
 
 def solution(mesh):

time: 483 us -> 356 us (0.74); the launches traced: 475 us -> 355 us
  matrix products: 116 us -> 5.48 us
  Pallas kernels: 308 us -> 330 us
  local copies, waits for them, and re-layouts: 34.5 us -> 14.6 us
  other arithmetic: 15.9 us -> 4.29 us
    dot_general x11 -> x0, matrix products: 110 us -> none  [the longest x1 21.7 us: per_device(): jnp.einsum('hqk,khe->qhe', score_grad, key_half, preferred_element_type=j...]
    pallas_call x2, Pallas kernels: 202 us -> 224 us  [the longest x1 128 us: forward(): pl.pallas_call(forward_kernel, out_shape=(jax.ShapeDtypeStruct((group_row...]
    dot_general x2 -> x0, local copies, waits for them, and re-layouts: 17.7 us -> none  [the longest x1 9.04 us: per_device(): jnp.einsum('qd,qc->dc', group_x, projected_grad, preferred_element_type=j...]
where the time goes in v2:
time: 356 us; the launch traced here: 355 us
  Pallas kernels  330 us (93%)
  local copies, waits for them, and re-layouts  14.6 us (4%)
  matrix products  5.48 us (2%)
  other arithmetic  4.29 us (1%)
    pallas_call x1, Pallas kernels, forward(): pl.pallas_call(forward_kernel, out_shape=(jax.ShapeDtypeStruct((group_row...  128 us
    pallas_call x1, Pallas kernels, gather_all(): pl.pallas_call(gather_kernel, out_shape=(jax.ShapeDtypeStruct((rows * 4,...  107 us
    pallas_call x1, Pallas kernels, backward(): pl.pallas_call(backward_kernel, out_shape=(jax.ShapeDtypeStruct((2, 48, Q...  95.7 us

profile of v2, /device:TPU:16, one launch (start us, length us, event | category | flops | bytes accessed | tf_op | source)
XLA Modules:
  0.0 355.3 jit_solution(9697271720945549424)
XLA Ops:
  0.6 0.8 fusion.11
  1.5 0.1 copy.14
  1.5 0.1 reduce-window.16
  1.6 0.1 reduce
  1.7 0.7 bitcast_subtract_fusion
  2.4 0.7 fusion.10
  3.1 0.1 fusion.3
  3.2 0.1 mul.89
  3.3 0.1 fusion.4
  3.4 0.1 lt.80
  3.5 0.1 add_select_fusion
  3.6 0.1 select_n.82
  3.7 2.7 convolution_convert_fusion
  6.4 1.6 fusion.7
  8.0 0.1 reduce.1
  8.2 0.1 convert_reduce_fusion
  8.3 0.7 gather_fusion
  9.0 0.1 add_select_fusion.1
  9.1 0.1 select_n.85
  9.2 0.8 fusion.chosen
  10.0 0.7 pad_maximum_fusion
  10.8 106.5 %gather_rows_weights.1 = (bf16[1024,3072]{1,0:T(8,128)(2,1)}, bf16[4,4,2,2,48,1536]{5,4,3,2,1,0:T(8,128)(2,1)}) custom-call(bf16[32,16,3072]{2,1,0:T(8,128)(2,1)} %bitcast.24, bf16[2,48,1536]{2,1,0:T(8,128)(2,1)} %bitcast.28, bf16[256,512]{1,0:T(8,128)(2,1)} %fusion.chosen), custom_call_target="tpu_custom_call" | custom-call | tf_op jit(solution)/shard_map/gather_rows_weights/pallas_call | solution.py:201
  117.3 2.8 constant_dynamic-slice_fusion.1.x_own
  120.1 2.8 convolution_convert_fusion.1
  122.9 0.1 fusion.5
  123.0 0.8 copy.16.weight
  123.8 1.1 select_convert_fusion
  124.9 127.9 %forward_residual_gradient.1 = (bf16[1024,3072]{1,0:T(8,128)(2,1)}, bf16[3,1024,256]{2,1,0:T(8,128)(2,1)}, bf16[3,1024,256]{2,1,0:T(8,128)(2,1)}, bf16[3,1024,12...) custom-call(bf16[32,16,3072]{2,1,0:T(8,128)(2,1)} %bitcast.25, ...), custom_call_target="tpu_custom_call" | custom-call | tf_op jit(solution)/shard_map/forward_residual_gradient/pallas_call | solution.py:390
  252.8 3.4 slice.6.w_out
  256.2 95.7 %backward_scatter.1 = (f32[2,48,1152]{2,1,0:T(8,128)}, f32[2,48,384]{2,1,0:T(8,128)}) custom-call(bf16[1024,3072]{1,0:T(8,128)(2,1)} %get-tuple-element.15.d_full, bf16[1024,3072]{1,0:T(8,128)(2,1)} %get-tuple-element.13.x_full, bf16[3072,384]{1,0:T(8,128)(2,1)} %slice.6.w_out, bf16[3,1024,256]{2,1,0:T(8,128)(2,1)} %get-tuple-element.16.q_marked, ...), custom_call_target="tpu_custom_call" | custom-call | tf_op jit(solution)/shard_map/backward_scatter/pallas_call | solution.py:641
  351.9 1.8 copy.19
  353.7 1.6 copy.20
  (24 shorter events, 0.2 us)
Async XLA Ops:
  0.6 3.0 copy-start
  3.7 6.3 %copy-start.2 = (bf16[96,1152]{1,0:T(8,128)(2,1)S(1)}, bf16[96,1152]{1,0:T(8,128)(2,1)}, u32[]{:S(2)}) copy-start(bf16[96,1152]{1,0:T(8,128)(2,1)} %param.12) | copy-start | bytes 663556
  3.7 6.3 %copy-start.3 = (bf16[96,384]{1,0:T(8,128)(2,1)S(1)}, bf16[96,384]{1,0:T(8,128)(2,1)}, u32[]{:S(2)}) copy-start(bf16[96,384]{1,0:T(8,128)(2,1)} %param.13) | copy-start | bytes 221188
  117.3 2.8 copy-start.1
  120.1 2.8 copy-start.4
  120.1 2.8 copy-start.5

commit v3 on v2

--- a/solution.py
+++ b/solution.py
@@ -34,6 +34,10 @@
 
 
 Z, X, Y, A, C = range(5)
+
+
+def chip_partner(place):
+    return moved(moved(place, Y, 1), A, 1)
 
 
 class Copies:
@@ -93,13 +97,13 @@
     return sent[2], sent[3], third_up, third_down
 
 
-def gather_kernel(packed, shard, chosen, x_full, w_full, received, own_rows, a2a_send, a2a_recv, send_sem, recv_sem, local_sem):
+def gather_kernel(packed, shard, chosen, labels, x_full, w_full, labels_there, received, own_rows, a2a_send, a2a_recv, send_sem, recv_sem, local_sem):
     me = my_place()
     z, x, y, a, c = me
     dp = lax.axis_index("dp")
     seq = lax.axis_index("seq")
     rows = own_rows.shape[0]
-    other_chip, other_core = moved(me, A, 1), moved(me, C, 1)
+    other_chip, other_core = chip_partner(me), moved(me, C, 1)
     barrier = pltpu.get_barrier_semaphore()
 
     @pl.loop(1, 32)
@@ -114,6 +118,7 @@
     own_shard = pltpu.make_async_copy(shard, w_full.at[z, x, y], local_sem.at[0])
     own_shard.start()
     across = copies.start(shard, w_full.at[z, x, y], moved(me, Y, 1))
+    labels_across = copies.start(labels, labels_there, moved(me, Y, 1))
 
     def block_copy(k):
         to = dp_peer(me, k, 1)
@@ -186,6 +191,7 @@
         for copy in rest[half]:
             copy.wait_recv()
     own_place.wait()
+    labels_across.wait_recv()
 
     @pl.loop(1, 32)
     def _(k):
@@ -194,35 +200,37 @@
     copies.finish()
 
 
-def gather_all(packed, shard, chosen):
+def gather_all(packed, shard, chosen, labels):
     rows = chosen.shape[0]
     width = packed.shape[2]
     w_cols = shard.shape[1]
-    x_full, w_full = pl.pallas_call(
+    x_full, w_full, labels_there = pl.pallas_call(
         gather_kernel,
         out_shape=(
             jax.ShapeDtypeStruct((rows * 4, width), jnp.bfloat16),
             jax.ShapeDtypeStruct((4, 4, 2, 2, 48, w_cols), jnp.bfloat16),
+            jax.ShapeDtypeStruct(labels.shape, labels.dtype),
         ),
         in_specs=[
             pl.BlockSpec(memory_space=pl.ANY),
             pl.BlockSpec(memory_space=pl.ANY),
             pl.BlockSpec(memory_space=pltpu.VMEM),
+            pl.BlockSpec(memory_space=pl.ANY),
         ],
-        out_specs=(pl.BlockSpec(memory_space=pl.ANY), pl.BlockSpec(memory_space=pl.ANY)),
+        out_specs=(pl.BlockSpec(memory_space=pl.ANY),) * 3,
         scratch_shapes=[
             pltpu.VMEM(packed.shape, jnp.bfloat16),
             pltpu.VMEM((rows, width), jnp.bfloat16),
             pltpu.SemaphoreType.DMA((32,)),
             pltpu.SemaphoreType.DMA((32,)),
-            pltpu.SemaphoreType.DMA((28,)),
-            pltpu.SemaphoreType.DMA((28,)),
+            pltpu.SemaphoreType.DMA((29,)),
+            pltpu.SemaphoreType.DMA((29,)),
             pltpu.SemaphoreType.DMA((3,)),
         ],
         compiler_params=pltpu.CompilerParams(collective_id=1, has_side_effects=True, vmem_limit_bytes=VMEM_LIMIT),
         name="gather_rows_weights",
-    )(packed, shard.reshape(2, 48, w_cols), chosen)
-    return x_full, w_full.reshape(3072, w_cols)
+    )(packed, shard.reshape(2, 48, w_cols), chosen, labels)
+    return x_full, w_full.reshape(3072, w_cols), labels_there
 
 
 CHUNKS = 4
@@ -245,16 +253,16 @@
 
 
 def forward_kernel(
-    packed, chosen, x_full, w_full, mark_q, mark_k, x_own, weight,
+    packed, chosen, x_full, w_full, mark_q, mark_k, weight,
     d_full, q_marked, k_marked, v_half, factors, inverse, mixed,
     projected, v_turned, partial, received, target, from_core, summed, from_chip,
     a2a_send, a2a_recv, send_sem, recv_sem, local_sem,
 ):
     me = my_place()
     dp = lax.axis_index("dp")
-    rows, width = x_own.shape
-    group_rows = x_full.shape[0]
-    other_chip, other_core = moved(me, A, 1), moved(me, C, 1)
+    rows = weight.shape[0]
+    group_rows, width = x_full.shape
+    other_chip, other_core = chip_partner(me), moved(me, C, 1)
     barrier = pltpu.get_barrier_semaphore()
 
     @pl.loop(1, 32)
@@ -361,7 +369,7 @@
         at = pl.ds(chunk * step, step)
         mine = rows_of(me, chunk)
         prediction = (
-            x_own[at].astype(jnp.float32)
+            x_full[mine].astype(jnp.float32)
             + (partial[mine].astype(jnp.float32) + from_core[1, at].astype(jnp.float32) + from_chip[at].astype(jnp.float32))
         )
         d_full[mine] = (weight[at] * (prediction - target[at].astype(jnp.float32))).astype(jnp.bfloat16)
@@ -382,9 +390,9 @@
     copies.finish()
 
 
-def forward(packed, chosen, x_full, w_full, mark_q, mark_k, x_own, weight):
-    rows, width = x_own.shape
-    group_rows = x_full.shape[0]
+def forward(packed, chosen, x_full, w_full, mark_q, mark_k, weight):
+    rows = weight.shape[0]
+    group_rows, width = x_full.shape
     vmem = pl.BlockSpec(memory_space=pltpu.VMEM)
     half, full = jnp.bfloat16, jnp.float32
     return pl.pallas_call(
@@ -398,7 +406,7 @@
             jax.ShapeDtypeStruct((HEADS, group_rows, HD), full),
             jax.ShapeDtypeStruct((group_rows, OUT), half),
         ),
-        in_specs=[pl.BlockSpec(memory_space=pl.ANY)] + [vmem] * 7,
+        in_specs=[pl.BlockSpec(memory_space=pl.ANY)] + [vmem] * 6,
         out_specs=(vmem,) * 7,
         scratch_shapes=[
             pltpu.VMEM((rows, QKV), full),
@@ -417,7 +425,7 @@
         ],
         compiler_params=pltpu.CompilerParams(collective_id=2, has_side_effects=True, vmem_limit_bytes=VMEM_LIMIT),
         name="forward_residual_gradient",
-    )(packed, chosen, x_full, w_full, mark_q, mark_k, x_own, weight)
+    )(packed, chosen, x_full, w_full, mark_q, mark_k, weight)
 
 
 def added(*values):
@@ -475,13 +483,15 @@
 
 
 def backward_kernel(
-    d_full, x_full, w_out, q_marked, k_marked, v_half, factors, inverse, mixed,
+    d_full, x_full, weights, q_marked, k_marked, v_half, factors, inverse, mixed,
     qkv_sums, out_sums,
     d_out, k_turned, dq, dk, dv, d_proj,
-    grads, got_far, sum_far, half_far, got_near, sum_near, half_near, got_last, send_sem, recv_sem,
+    grads, got_far, sum_far, half_far, got_near, sum_near, half_near, got_last, w_out, send_sem, recv_sem, local_sem,
 ):
     me = my_place()
     z, x, y, a, c = me
+    w_copy = pltpu.make_async_copy(weights.at[:, QKV:QKV + OUT], w_out, local_sem.at[0])
+    w_copy.start()
     greet([moved(me, Z, 1), moved(me, Z, -1), moved(me, X, 1), moved(me, X, -1), moved(me, Y, 1)])
     copies = Copies(send_sem, recv_sem)
     far_axis, near_axis = (X, Z), (Z, X)
@@ -594,6 +604,7 @@
     slabs = [Slab(h) for h in range(HEADS)]
     weight_grads(HEADS, d_full, mixed)
     out_slab.far_start()
+    w_copy.wait()
 
     @pl.loop(0, 4)
     def _(i):
@@ -634,8 +645,8 @@
     copies.finish()
 
 
-def backward(d_full, x_full, w_out, q_marked, k_marked, v_half, factors, inverse, mixed):
-    group_rows = x_full.shape[0]
+def backward(d_full, x_full, weights, q_marked, k_marked, v_half, factors, inverse, mixed):
+    group_rows, width = x_full.shape
     half = lambda *lead: pltpu.VMEM((SLABS, 2, *lead, 48, 3 * HD), jnp.bfloat16)
     vmem = pl.BlockSpec(memory_space=pltpu.VMEM)
     qkv_sums, out_sums = pl.pallas_call(
@@ -644,7 +655,7 @@
             jax.ShapeDtypeStruct((2, 48, QKV), jnp.float32),
             jax.ShapeDtypeStruct((2, 48, OUT), jnp.float32),
         ),
-        in_specs=[vmem] * 9,
+        in_specs=[vmem] * 2 + [pl.BlockSpec(memory_space=pl.ANY)] + [vmem] * 6,
         out_specs=(vmem, vmem),
         scratch_shapes=[
             pltpu.VMEM((group_rows, OUT), jnp.bfloat16),
@@ -661,12 +672,14 @@
             half(2),
             half(2),
             half(),
+            pltpu.VMEM((width, OUT), jnp.bfloat16),
             pltpu.SemaphoreType.DMA((26 * SLABS,)),
             pltpu.SemaphoreType.DMA((26 * SLABS,)),
+            pltpu.SemaphoreType.DMA((1,)),
         ],
         compiler_params=pltpu.CompilerParams(collective_id=3, has_side_effects=True, vmem_limit_bytes=VMEM_LIMIT),
         name="backward_scatter",
-    )(d_full, x_full, w_out, q_marked, k_marked, v_half, factors, inverse, mixed)
+    )(d_full, x_full, weights, q_marked, k_marked, v_half, factors, inverse, mixed)
     return qkv_sums.reshape(96, QKV), out_sums.reshape(96, OUT)
 
 
@@ -679,12 +692,18 @@
 def per_device(clip_rows, velocity_target, plan, segment_ids, reward_levels, w_qkv, w_out):
     groups = lax.axis_size("dp")
     shards = lax.axis_size("seq")
-    group = lax.axis_index("dp")
+    place = lax.axis_index("dp")
     shard = lax.axis_index("seq")
+    crossed = shard // 2
+    group = place ^ crossed
     rows_dev, width = clip_rows.shape
-    group_rows = rows_dev * shards
-    counts = plan[group, shard]
+    counts = plan[place, shard]
     send_start = jnp.cumsum(counts) - counts
+
+    def by_device(values):
+        return jnp.where(crossed == 1, values.reshape(-1, 2)[:, ::-1].reshape(-1), values)
+
+    counts, send_start = by_device(counts), by_device(send_start)
     slot_index = jnp.arange(CAP, dtype=jnp.int32)
     source_block = jnp.where(slot_index[None, :] < counts[:, None], send_start[:, None] + slot_index[None, :], -1).reshape(-1)
     pack = spread(source_block, rows_dev * CAP, rows_dev)
@@ -700,10 +719,15 @@
     flat_slot = source_group * CAP + slot_ids - arriving_start
     chosen = spread(flat_slot, rows_dev, rows_dev * CAP)
 
-    group_x, weights = gather_all(packed(clip_rows), jnp.concatenate([w_qkv, w_out], axis=1), chosen)
-    segment_row = segment_ids[0]
+    segments = segment_ids.shape[1]
+    labels = jnp.concatenate([segment_ids, jnp.pad(reward_levels, ((0, 0), (0, HD - reward_levels.shape[1])))], axis=1)
+    labels = jnp.broadcast_to(labels, (8, segments + HD))
+    group_x, weights, labels_there = gather_all(
+        packed(clip_rows), jnp.concatenate([w_qkv, w_out], axis=1), chosen, labels)
+    labels = jnp.where(crossed == 1, labels_there, labels)[0]
+    segment_row = labels[:segments]
     clip_index = jnp.arange(reward_levels.shape[1], dtype=jnp.int32)
-    levels = reward_levels[0].astype(jnp.float32) / 8.0
+    levels = labels[segments:segments + reward_levels.shape[1]].astype(jnp.float32) / 8.0
     own_segment = lax.dynamic_slice(segment_row, (shard * rows_dev,), (rows_dev,))
     row_weight = jnp.sum(
         jnp.where(own_segment[:, None] == clip_index[None, :], levels[None, :], jnp.float32(0.0)),
@@ -711,7 +735,6 @@
         keepdims=True,
     )
     loss_scale = 1.0 / math.sqrt(rows_dev * groups * shards)
-    own_x = lax.dynamic_slice(group_x, (shard * rows_dev, 0), (rows_dev, width))
 
     sign = (2 * segment_row - 1)[:, None]
     lane = jnp.arange(HD, dtype=jnp.int32)[None, :]
@@ -719,8 +742,8 @@
     mark_k = jnp.where(lane == 0, 32 * sign, jnp.where(lane == 1, 32, 0)).astype(jnp.bfloat16)
 
     pred_grad, *saved = forward(
-        packed(velocity_target), chosen, group_x, weights, mark_q, mark_k, own_x, row_weight * loss_scale)
-    return backward(pred_grad, group_x, weights[:, QKV:], *saved)
+        packed(velocity_target), chosen, group_x, weights, mark_q, mark_k, row_weight * loss_scale)
+    return backward(pred_grad, group_x, weights, *saved)
 
 
 def solution(mesh):

time: 356 us -> 327 us (0.919)
  Pallas kernels: 330 us -> 301 us
  local copies, waits for them, and re-layouts: 14.6 us -> 9.97 us
    pallas_call x1, Pallas kernels: 128 us -> 107 us  [forward(): pl.pallas_call(forward_kernel, out_shape=(jax.ShapeDtypeStruct((group_row...]
    pallas_call x1, Pallas kernels: 95.7 us -> 87.9 us  [backward(): pl.pallas_call(backward_kernel, out_shape=(jax.ShapeDtypeStruct((2, 48, Q...]
where the time goes in v3:
time: 327 us; the launch traced here: 323 us
  Pallas kernels  301 us (92%)
  local copies, waits for them, and re-layouts  9.97 us (3%)
  other arithmetic  6.11 us (2%)
  matrix products  5.38 us (2%)
    pallas_call x1, Pallas kernels, forward(): pl.pallas_call(forward_kernel, out_shape=(jax.ShapeDtypeStruct((group_row...  107 us
    pallas_call x1, Pallas kernels, gather_all(): pl.pallas_call(gather_kernel, out_shape=(jax.ShapeDtypeStruct((rows * 4,...  106 us
    pallas_call x1, Pallas kernels, backward(): pl.pallas_call(backward_kernel, out_shape=(jax.ShapeDtypeStruct((2, 48, Q...  87.9 us

profile of v3, /device:TPU:16, one launch (start us, length us, event | category | flops | bytes accessed | tf_op | source)
XLA Modules:
  0.0 323.1 jit_solution(1524762105270312882)
XLA Ops:
  0.7 0.5 broadcast.196
  1.2 1.3 fusion.11
  2.5 0.1 reshape_squeeze.3
  2.6 0.7 fusion.5
  3.4 0.1 reshape.208
  3.5 1.6 fusion.10
  5.2 0.1 reduce.3
  5.3 0.1 convert_reduce_fusion
  5.4 0.7 gather_fusion
  6.2 0.1 select_n.124
  6.3 0.1 copy.14
  6.5 0.1 reduce.1
  6.6 0.1 reshape.209
  6.8 0.1 reshape.210
  6.9 0.1 lt.75
  7.1 0.1 mul.88
  7.3 0.1 add_select_fusion
  7.3 0.1 select_n.120
  7.4 0.6 broadcast_in_dim.119.labels
  8.1 0.8 fusion.chosen
  8.9 1.7 pad_maximum_fusion
  10.6 2.7 convolution_convert_fusion
  13.3 2.7 convolution_convert_fusion.1
  16.0 105.7 %gather_rows_weights.1 = (bf16[1024,3072]{1,0:T(8,128)(2,1)}, bf16[4,4,2,2,48,1536]{5,4,3,2,1,0:T(8,128)(2,1)}, s32[8,1152]{1,0:T(8,128)}) custom-call(bf16[32,16,3072]{2,1,0:T(8,128)(2,1)} %bitcast.28, bf16[2,48,1536]{2,1,0:T(8,128)(2,1)} %bitcast.29, bf16[256,512]{1,0:T(8,128)(2,1)} %fusion.chosen, s32[8,1152]{1,0:T(8,128)} %broadcast_in_dim.119.labels), custom_call_target="tpu_custom_call" | custom-call | tf_op jit(solution)/shard_map/gather_rows_weights/pallas_call | solution.py:207
  121.7 0.8 broadcast_select_fusion
  122.5 0.1 fusion.6
  122.6 0.8 copy.16.weight
  123.4 1.1 select_convert_fusion
  124.6 107.3 %forward_residual_gradient.1 = (bf16[1024,3072]{1,0:T(8,128)(2,1)}, bf16[3,1024,256]{2,1,0:T(8,128)(2,1)}, bf16[3,1024,256]{2,1,0:T(8,128)(2,1)}, bf16[3,1024,12...) custom-call(bf16[32,16,3072]{2,1,0:T(8,128)(2,1)} %bitcast.27, ...), custom_call_target="tpu_custom_call" | custom-call | tf_op jit(solution)/shard_map/forward_residual_gradient/pallas_call | solution.py:398
  231.9 87.9 %backward_scatter.1 = (f32[2,48,1152]{2,1,0:T(8,128)}, f32[2,48,384]{2,1,0:T(8,128)}) custom-call(bf16[1024,3072]{1,0:T(8,128)(2,1)} %get-tuple-element.17.d_full, bf16[1024,3072]{1,0:T(8,128)(2,1)} %get-tuple-element.14.x_full, bf16[3072,1536]{1,0:T(8,128)(2,1)} %bitcast.26, bf16[3,1024,256]{2,1,0:T(8,128)(2,1)} %get-tuple-element.18.q_marked, ...), custom_call_target="tpu_custom_call" | custom-call | tf_op jit(solution)/shard_map/backward_scatter/pallas_call | solution.py:652
  319.7 1.8 copy.19
  321.5 1.6 copy.20
  (24 shorter events, 0.6 us)
Async XLA Ops:
  0.6 9.9 %copy-start = (bf16[256,3072]{1,0:T(8,128)(2,1)S(1)}, bf16[256,3072]{1,0:T(8,128)(2,1)}, u32[]{:S(2)}) copy-start(bf16[256,3072]{1,0:T(8,128)(2,1)} %param.7) | copy-start | bytes 4718596
  10.6 2.7 copy-start.1

commit v4 on v3

v4 whole, which is shorter than its diff:
```python
import math

import jax
import jax.numpy as jnp
from jax import lax
from jax.experimental import pallas as pl
from jax.experimental.pallas import tpu as pltpu
from jax.sharding import PartitionSpec as P

HD = 128
CAP = 2
MESH = pl.DeviceIdType.MESH
VMEM_LIMIT = 60 * 1024 * 1024

epsilon = 1e-06


def my_place():
    dp = lax.axis_index("dp")
    seq = lax.axis_index("seq")
    return (dp // 8, (dp // 2) % 4, dp % 2, seq // 2, seq % 2)


def device(place):
    z, x, y, a, c = place
    return {"dp": z * 8 + x * 2 + y, "seq": a * 2 + c}


def moved(place, axis, by):
    place = list(place)
    size = (4, 4, 2, 2, 2)[axis]
    place[axis] = (place[axis] + by + size) % size
    return tuple(place)


Z, X, Y, A, C = range(5)


def chip_partner(place):
    return moved(moved(place, Y, 1), A, 1)


class Copies:
    def __init__(self, send_sem, recv_sem):
        self.send_sem, self.recv_sem, self.used = send_sem, recv_sem, 0
        self.started = []

    def start(self, src, dst, to):
        copy = pltpu.make_async_remote_copy(
            src_ref=src,
            dst_ref=dst,
            send_sem=self.send_sem.at[self.used],
            recv_sem=self.recv_sem.at[self.used],
            device_id=device(to),
            device_id_type=MESH,
        )
        self.used += 1
        copy.start()
        self.started.append(copy)
        return copy

    def finish(self):
        for copy in self.started:
            copy.wait_send()


def greet(places):
    barrier = pltpu.get_barrier_semaphore()
    for place in places:
        pl.semaphore_signal(barrier, inc=1, device_id=device(place), device_id_type=MESH)
    pl.semaphore_wait(barrier, len(places))


def dp_peer(place, k, sign):
    z, x, y, a, c = place
    dz, dx, dy = k // 8, (k // 2) % 4, k % 2
    return ((z + sign * dz + 4) % 4, (x + sign * dx + 4) % 4, (y + sign * dy + 2) % 2, a, c)


def ring_gather_start(copies, me, axis, part):
    own = me[axis]
    up, down = moved(me, axis, 1), moved(me, axis, -1)
    first_up = copies.start(part(own, 0), part(own, 0), up)
    first_down = copies.start(part(own, 1), part(own, 1), down)
    second_up = copies.start(part(own, 1), part(own, 1), up)
    second_down = copies.start(part(own, 0), part(own, 0), down)
    return first_up, first_down, second_up, second_down


def ring_gather_forward(copies, me, axis, part, sent):
    up, down = moved(me, axis, 1), moved(me, axis, -1)
    below, above = down[axis], up[axis]
    sent[0].wait_recv()
    third_up = copies.start(part(below, 0), part(below, 0), up)
    sent[1].wait_recv()
    third_down = copies.start(part(above, 1), part(above, 1), down)
    return sent[2], sent[3], third_up, third_down


CHUNKS = 4
HEADS = 3
QKV = HEADS * 3 * HD
OUT = HEADS * HD
SLABS = HEADS + 1
EXP2_SCALE = math.log2(math.e) / math.sqrt(HD)


def nt(left, right):
    return lax.dot_general(left, right, (((1,), (1,)), ((), ())), preferred_element_type=jnp.float32)


def tn(left, right):
    return lax.dot_general(left, right, (((0,), (0,)), ((), ())), preferred_element_type=jnp.float32)


def nn(left, right):
    return jnp.dot(left, right, preferred_element_type=jnp.float32)


MOVES = 2


def forward_kernel(
    packed, shard_qkv, shard_out, labels, chosen, pack, own_target,
    d_full, x_out, w_out, q_out, k_out, v_out, factors_out, inverse_out, mixed_out,
    w_full, x_full, received, packed_target, received_target, labels_there,
    q_marked, k_marked, v_half, v_turned, factors, inverse, mixed,
    partial, target, from_core, from_chip, d_own,
    a2a_send, a2a_recv, send_sem, recv_sem, local_sem,
):
    me = my_place()
    z, x, y, a, c = me
    dp = lax.axis_index("dp")
    rows, width = own_target.shape
    group_rows = x_full.shape[0]
    other_chip, other_core = chip_partner(me), moved(me, C, 1)
    barrier = pltpu.get_barrier_semaphore()

    @pl.loop(1, 32)
    def _(k):
        pl.semaphore_signal(barrier, inc=1, device_id=device(dp_peer(me, k, 1)), device_id_type=MESH)

    for place in (other_chip, other_core):
        pl.semaphore_signal(barrier, inc=1, device_id=device(place), device_id_type=MESH)

    locals_started = []

    def local_copy(src, dst):
        copy = pltpu.make_async_copy(src, dst, local_sem.at[len(locals_started)])
        copy.start()
        locals_started.append(copy)
        return copy

    shards = [
        local_copy(shard_qkv.at[:, :, h * 3 * HD:(h + 1) * 3 * HD], w_full.at[h, z, x, y]) for h in range(HEADS)
    ] + [local_copy(shard_out, w_full.at[HEADS, z, x, y])]
    own_block = local_copy(packed.at[dp], received.at[dp])
    for copy in shards:
        copy.wait()
    pl.semaphore_wait(barrier, 33)

    copies = Copies(send_sem, recv_sem)
    across = copies.start(w_full.at[:, z, x, y], w_full.at[:, z, x, y], moved(me, Y, 1))
    labels_across = copies.start(labels, labels_there, moved(me, Y, 1))

    def block_copy(which, src, dst, k):
        to = dp_peer(me, k, 1)
        return pltpu.make_async_remote_copy(
            src_ref=src.at[device(to)["dp"]],
            dst_ref=dst.at[dp],
            send_sem=a2a_send.at[which, k],
            recv_sem=a2a_recv.at[which, k],
            device_id=device(to),
            device_id_type=MESH,
        )

    @pl.loop(1, 32)
    def _(k):
        block_copy(0, packed, received, k).start()

    tile = 512

    @pl.loop(0, width // tile)
    def _(t):
        columns = pl.ds(pl.multiple_of(t * tile, tile), tile)
        blocks = nn(pack[...], own_target[:, columns]).astype(jnp.bfloat16)
        packed_target[:, :, columns] = blocks.reshape(packed_target.shape[0], packed_target.shape[1], tile)

    def select(src, dst):
        @pl.loop(0, width // tile)
        def _(t):
            columns = pl.ds(pl.multiple_of(t * tile, tile), tile)
            blocks = src[:, :, columns].reshape(rows * CAP, tile)
            dst[:, columns] = nn(chosen[...], blocks).astype(jnp.bfloat16)

    def near(half):
        if half == 0:
            return lambda at, which: w_full.at[:, at, x, which, 0]
        return lambda at, which: w_full.at[:, z, at, which, 1]

    def far(s, half):
        if half == 0:
            return lambda at, which: w_full.at[s, pl.ds(2 * which, 2), at, :, 0]
        return lambda at, which: w_full.at[s, at, pl.ds(2 * which, 2), :, 1]

    near_axis, far_axis = (Z, X), (X, Z)
    across.wait_recv()
    sent = [ring_gather_start(copies, me, near_axis[half], near(half)) for half in (0, 1)]
    rest = [ring_gather_forward(copies, me, near_axis[half], near(half), sent[half]) for half in (0, 1)]
    for half in (0, 1):
        for copy in rest[half]:
            copy.wait_recv()

    far_sent = {}

    def far_start(s):
        far_sent[s] = [ring_gather_start(copies, me, far_axis[half], far(s, half)) for half in (0, 1)]

    def far_forward(s):
        far_sent[s] = [ring_gather_forward(copies, me, far_axis[half], far(s, half), far_sent[s][half]) for half in (0, 1)]

    def far_wait(s):
        for half in (0, 1):
            for copy in far_sent[s][half]:
                copy.wait_recv()

    far_start(0)

    def rows_of(place, chunk=0, chunks=1):
        step = rows // chunks
        return pl.ds(pl.multiple_of(device(place)["seq"] * rows + chunk * step, step), step)

    own_block.wait()

    @pl.loop(1, 32)
    def _(k):
        block_copy(0, packed, received, k).wait_recv()

    select(received, x_full.at[rows_of(me)])
    x_chip = []
    for chunk in range(MOVES):
        at = rows_of(me, chunk, MOVES)
        x_chip.append(copies.start(x_full.at[at], x_full.at[at], other_chip))
    x_core = copies.start(x_full.at[rows_of(me)], x_full.at[rows_of(me)], other_core)
    far_start(1)

    labels_across.wait_recv()
    lane = lax.broadcasted_iota(jnp.int32, (rows, HD), 1)
    for i in range(group_rows // rows):
        at = slice(i * rows, (i + 1) * rows)
        segment = jnp.where(a == 1, labels_there[0:1, at], labels[0:1, at]).astype(jnp.float32)
        sign = jnp.broadcast_to(2.0 * segment - 1.0, (HD, rows)).T
        mark_q = jnp.where(lane == 0, 64.0 * sign, jnp.where(lane == 1, -64.0, 0.0)).astype(jnp.bfloat16)
        mark_k = jnp.where(lane == 0, 32.0 * sign, jnp.where(lane == 1, 32.0, 0.0)).astype(jnp.bfloat16)
        for h in range(HEADS):
            q_marked[h, at, HD:2 * HD] = mark_q
            k_marked[h, at, HD:2 * HD] = mark_k

    def project(h, chip):
        @pl.loop(0, 2)
        def _(i):
            at = pl.ds(pl.multiple_of((chip * 2 + i) * rows, rows), rows)
            raw = nn(x_full[at, :], w_full[h].reshape(width, 3 * HD))
            for part, marked in ((0, q_marked), (1, k_marked)):
                values = raw[:, part * HD:(part + 1) * HD]
                factor = lax.rsqrt(jnp.mean(values * values, axis=-1, keepdims=True) + epsilon)
                marked[h, at, 0:HD] = (values * factor).astype(jnp.bfloat16)
                factors[part, h, at, :] = jnp.broadcast_to(factor, (rows, HD))
            values = raw[:, 2 * HD:3 * HD]
            v_half[h, at, :] = values.astype(jnp.bfloat16)
            v_turned[h, :, at] = values.T.astype(jnp.bfloat16)

    def attend(h, at):
        scores = nt(k_marked[h], q_marked[h, at, :])
        raised = jnp.exp2(scores * EXP2_SCALE)
        inverse_sum = 1.0 / jnp.sum(raised, axis=0, keepdims=True)
        turned = nn(v_turned[h], raised.astype(jnp.bfloat16)) * inverse_sum
        mixed[at, h * HD:(h + 1) * HD] = turned.T.astype(jnp.bfloat16)
        inverse[h, at, :] = jnp.broadcast_to(inverse_sum, (HD, rows)).T

    def attend_all(h):
        @pl.loop(0, group_rows // rows)
        def _(i):
            attend(h, pl.ds(pl.multiple_of(i * rows, rows), rows))

    x_passed = []

    def x_pass(chunk):
        x_chip[chunk].wait_recv()
        at = rows_of(other_chip, chunk, MOVES)
        x_passed.append(copies.start(x_full.at[at], x_full.at[at], other_core))

    far_forward(0)
    x_core.wait_recv()
    far_wait(0)
    far_start(2)
    project(0, a)
    x_pass(0)
    far_forward(1)
    far_wait(1)
    far_start(3)
    project(1, a)
    far_forward(2)
    x_pass(1)
    far_wait(2)
    project(2, a)
    far_forward(3)

    @pl.loop(1, 32)
    def _(k):
        block_copy(1, packed_target, received_target, k).start()

    own_block = local_copy(packed_target.at[dp], received_target.at[dp])
    for copy in x_passed:
        copy.wait_recv()
    outs = [local_copy(x_full, x_out)]
    project(0, 1 - a)
    attend_all(0)
    project(1, 1 - a)
    attend_all(1)
    project(2, 1 - a)
    for src, dst in ((q_marked, q_out), (k_marked, k_out), (v_half, v_out), (factors, factors_out)):
        outs.append(local_copy(src, dst))
    far_wait(3)
    outs.append(local_copy(w_full.at[HEADS], w_out))

    def block(place):
        at = rows_of(place)
        attend(HEADS - 1, at)

        @pl.loop(0, 8)
        def _(t):
            weights = w_full[HEADS, t // 2, pl.ds(t % 2 * 2, 2)].reshape(3 * HD, OUT)
            columns = pl.ds(pl.multiple_of(t * 3 * HD, 3 * HD), 3 * HD)
            partial[at, columns] = nt(mixed[at, :], weights).astype(jnp.bfloat16)

    core_first, core_second, chip_sums = [], [], []
    step = rows // CHUNKS
    far_core = moved(other_chip, C, 1)
    block(far_core)
    for chunk in range(CHUNKS):
        core_first.append(copies.start(
            partial.at[rows_of(far_core, chunk, CHUNKS)], from_core.at[0, pl.ds(chunk * step, step)], other_core))
    block(other_chip)
    for chunk in range(CHUNKS):
        core_first[chunk].wait_recv()
        at = pl.ds(chunk * step, step)
        from_core[0, at] = (
            partial[rows_of(other_chip, chunk, CHUNKS)].astype(jnp.float32) + from_core[0, at].astype(jnp.float32)
        ).astype(jnp.bfloat16)
        chip_sums.append(copies.start(from_core.at[0, at], from_chip.at[at], other_chip))
    block(other_core)
    for chunk in range(CHUNKS):
        core_second.append(copies.start(
            partial.at[rows_of(other_core, chunk, CHUNKS)], from_core.at[1, pl.ds(chunk * step, step)], other_core))
    block(me)
    for src, dst in ((inverse, inverse_out), (mixed, mixed_out)):
        outs.append(local_copy(src, dst))

    own_block.wait()

    @pl.loop(1, 32)
    def _(k):
        block_copy(1, packed_target, received_target, k).wait_recv()

    select(received_target, target)
    own_lanes = rows_of(me)
    segment = jnp.where(a == 1, labels_there[0:1, own_lanes], labels[0:1, own_lanes]).astype(jnp.float32)
    first, second = (
        jnp.where(a == 1, labels_there[0:1, at:at + 1], labels[0:1, at:at + 1]).astype(jnp.float32)
        for at in (group_rows, group_rows + 1))
    loss_scale = 1.0 / math.sqrt(group_rows * 32)
    weight = (jnp.where(segment == 0.0, first, second) / 8.0) * loss_scale
    weight = jnp.broadcast_to(weight, (HD, rows)).T[:, 0:1]

    to_chip, to_core, passed = [], [], []
    for chunk in range(CHUNKS):
        core_second[chunk].wait_recv()
        chip_sums[chunk].wait_recv()
        at = slice(chunk * step, (chunk + 1) * step)
        mine = rows_of(me, chunk, CHUNKS)
        prediction = (
            x_full[mine].astype(jnp.float32)
            + (partial[mine].astype(jnp.float32) + from_core[1, at].astype(jnp.float32) + from_chip[at].astype(jnp.float32))
        )
        d_own[at] = (weight[at] * (prediction - target[at].astype(jnp.float32))).astype(jnp.bfloat16)
        to_chip.append(copies.start(d_own.at[at], d_full.at[mine], other_chip))
        to_core.append(copies.start(d_own.at[at], d_full.at[mine], other_core))
    outs.append(local_copy(d_own, d_full.at[rows_of(me)]))
    for chunk in range(CHUNKS):
        to_chip[chunk].wait_recv()
        theirs = rows_of(other_chip, chunk, CHUNKS)
        passed.append(copies.start(d_full.at[theirs], d_full.at[theirs], other_core))
    for chunk in range(CHUNKS):
        to_core[chunk].wait_recv()
        passed[chunk].wait_recv()

    @pl.loop(1, 32)
    def _(k):
        block_copy(0, packed, received, k).wait_send()
        block_copy(1, packed_target, received_target, k).wait_send()

    for copy in outs:
        copy.wait()
    copies.finish()


def forward(packed, shard_qkv, shard_out, labels, chosen, pack, own_target):
    rows, width = own_target.shape
    group_rows = rows * 4
    vmem = pl.BlockSpec(memory_space=pltpu.VMEM)
    hbm = pl.BlockSpec(memory_space=pl.ANY)
    half, full = jnp.bfloat16, jnp.float32
    saved = [
        ((HEADS, group_rows, 2 * HD), half),
        ((HEADS, group_rows, 2 * HD), half),
        ((HEADS, group_rows, HD), half),
        ((2, HEADS, group_rows, HD), full),
        ((HEADS, group_rows, HD), full),
        ((group_rows, OUT), half),
    ]
    q_shape, k_shape, v_shape, factors_shape, inverse_shape, mixed_shape = saved
    scratch = [
        ((SLABS, 4, 4, 2, 2, 48, 3 * HD), half),
        ((group_rows, width), half),
        (packed.shape, half),
        (packed.shape, half),
        (packed.shape, half),
        (labels.shape, labels.dtype),
        q_shape,
        k_shape,
        v_shape,
        ((HEADS, HD, group_rows), half),
        factors_shape,
        inverse_shape,
        mixed_shape,
        ((group_rows, width), half),
        ((rows, width), half),
        ((2, rows, width), half),
        ((rows, width), half),
        ((rows, width), half),
    ]
    sems = 6 + 12 + 12 * SLABS + 2 * MOVES + 1 + 6 * CHUNKS
    return pl.pallas_call(
        forward_kernel,
        out_shape=tuple(
            jax.ShapeDtypeStruct(*shape)
            for shape in [((group_rows, width), half), ((group_rows, width), half), ((4, 4, 2, 2, 48, OUT), half)] + saved
        ),
        in_specs=[hbm] * 3 + [vmem] * 4,
        out_specs=(hbm,) * 9,
        scratch_shapes=[pltpu.VMEM(*shape) for shape in scratch] + [
            pltpu.SemaphoreType.DMA((2, 32)),
            pltpu.SemaphoreType.DMA((2, 32)),
            pltpu.SemaphoreType.DMA((sems,)),
            pltpu.SemaphoreType.DMA((sems,)),
            pltpu.SemaphoreType.DMA((16,)),
        ],
        compiler_params=pltpu.CompilerParams(collective_id=2, has_side_effects=True, vmem_limit_bytes=VMEM_LIMIT),
        name="forward_residual_gradient",
    )(packed, shard_qkv.reshape(2, 48, QKV), shard_out.reshape(2, 48, OUT), labels, chosen, pack, own_target)


def added(*values):
    total = values[0].astype(jnp.float32)
    for value in values[1:]:
        total = total + value.astype(jnp.float32)
    return total


def reduce_start(copies, me, axis, block, got):
    up, down = moved(me, axis, 1), moved(me, axis, -1)
    opposite = moved(me, axis, 2)[axis]
    far_up = copies.start(block(opposite, 0), got(0), up)
    far_down = copies.start(block(opposite, 1), got(1), down)
    near_up = copies.start(block(up[axis], 1), got(2), up)
    near_down = copies.start(block(down[axis], 0), got(3), down)
    return far_up, far_down, near_up, near_down


def reduce_pass(copies, me, axis, block, got, sums, sent, add):
    up, down = moved(me, axis, 1), moved(me, axis, -1)
    sent[0].wait_recv()
    add(sums(0), [block(up[axis], 0), got(0)])
    sum_up = copies.start(sums(0), got(4), up)
    sent[1].wait_recv()
    add(sums(1), [block(down[axis], 1), got(1)])
    sum_down = copies.start(sums(1), got(5), down)
    return sent[2], sent[3], sum_up, sum_down


def reduce_end(me, axis, block, got, out, sent, add):
    sent[1].wait_recv()
    sent[2].wait_recv()
    add(out(0), [block(me[axis], 0), got(3), got(4)])
    sent[0].wait_recv()
    sent[3].wait_recv()
    add(out(1), [block(me[axis], 1), got(2), got(5)])


def add_rows(out, parts):
    lead = out.shape[:-2]
    count = math.prod(lead)

    @pl.loop(0, count)
    def _(i):
        index, rest = [], i
        for size in reversed(lead):
            index.insert(0, rest % size)
            rest = rest // size
        index = tuple(index)
        out[index] = added(*[part[index] for part in parts]).astype(out.dtype)


def backward_kernel(
    d_full, x_full, w_out, q_marked, k_marked, v_half, factors, inverse, mixed,
    qkv_sums, out_sums,
    d_out, k_turned, dq, dk, dv, d_proj,
    grads, got_far, sum_far, half_far, got_near, sum_near, half_near, got_last, send_sem, recv_sem,
):
    me = my_place()
    z, x, y, a, c = me
    greet([moved(me, Z, 1), moved(me, Z, -1), moved(me, X, 1), moved(me, X, -1), moved(me, Y, 1)])
    copies = Copies(send_sem, recv_sem)
    far_axis, near_axis = (X, Z), (Z, X)
    group_rows, width = x_full.shape
    rows = group_rows // 4
    scale = 1.0 / math.sqrt(HD)

    class Slab:
        def __init__(self, s):
            self.s = s

        def far_block(self, half):
            if half == 0:
                return lambda at, which: grads.at[self.s, pl.ds(2 * which, 2), at, :, 0]
            return lambda at, which: grads.at[self.s, at, pl.ds(2 * which, 2), :, 1]

        def near_block(self, half):
            return lambda at, which: half_far.at[self.s, half, at, which]

        def slots(self, ref, half):
            return lambda j: ref.at[self.s, half, j]

        def far_out(self, half):
            return lambda which: half_far.at[self.s, half, pl.ds(2 * which, 2)]

        def near_out(self, half):
            return lambda which: half_near.at[self.s, half, pl.ds(which, 1)]

        def far_start(self):
            self.sent = [
                reduce_start(copies, me, far_axis[h], self.far_block(h), self.slots(got_far, h)) for h in (0, 1)]

        def far_pass(self):
            self.sent = [
                reduce_pass(copies, me, far_axis[h], self.far_block(h), self.slots(got_far, h),
                            self.slots(sum_far, h), self.sent[h], add_rows)
                for h in (0, 1)]

        def near_start(self):
            for h in (0, 1):
                reduce_end(me, far_axis[h], self.far_block(h), self.slots(got_far, h), self.far_out(h), self.sent[h], add_rows)
            self.sent = [
                reduce_start(copies, me, near_axis[h], self.near_block(h), self.slots(got_near, h)) for h in (0, 1)]

        def near_pass(self):
            self.sent = [
                reduce_pass(copies, me, near_axis[h], self.near_block(h), self.slots(got_near, h),
                            self.slots(sum_near, h), self.sent[h], near_add)
                for h in (0, 1)]

        def last_start(self):
            for h in (0, 1):
                reduce_end(me, near_axis[h], self.near_block(h), self.slots(got_near, h), self.near_out(h), self.sent[h], near_add)
            self.sent = [
                copies.start(half_near.at[self.s, h, 1 - y], got_last.at[self.s, h], moved(me, Y, 1)) for h in (0, 1)]

        def end(self):
            for h in (0, 1):
                self.sent[h].wait_recv()
                total = added(half_near[self.s, h, y], got_last[self.s, h])
                if self.s == HEADS:
                    out_sums[h] = total
                else:
                    qkv_sums[h, :, self.s * 3 * HD:(self.s + 1) * 3 * HD] = total

    def near_add(out, parts):
        out[...] = added(*[part[...] for part in parts]).astype(out.dtype).reshape(out.shape)

    def weight_grads(s, left, right):
        @pl.loop(0, 8)
        def _(t):
            columns = pl.ds(pl.multiple_of(t * 384, 384), 384)
            term = tn(left[:, columns], right[...]).astype(jnp.bfloat16)
            grads[s, t // 2, pl.ds(t % 2 * 2, 2)] = term.reshape(2, 2, 2, 48, 384)

    def head(h):
        head_columns = slice(h * HD, (h + 1) * HD)

        @pl.loop(0, 4)
        def _(i):
            at = pl.ds(pl.multiple_of(i * rows, rows), rows)
            k_turned[:, at] = k_marked[h, at, 0:HD].astype(jnp.float32).T.astype(jnp.bfloat16)

        dk[...] = jnp.zeros_like(dk)
        dv[...] = jnp.zeros_like(dv)

        @pl.loop(0, 4)
        def _(i):
            at = pl.ds(pl.multiple_of(i * rows, rows), rows)
            raised = jnp.exp2(nt(k_marked[h], q_marked[h, at, :]) * EXP2_SCALE)
            d_here = d_out[at, head_columns]
            delta = jnp.sum((d_here.astype(jnp.float32) * mixed[at, head_columns].astype(jnp.float32)).T, axis=0, keepdims=True)
            d_scores = (raised * (nt(v_half[h], d_here) - delta)).astype(jnp.bfloat16)
            dv[...] += nn(raised.astype(jnp.bfloat16), d_here)
            dk[...] += nn(d_scores, q_marked[h, at, 0:HD])
            dq[at, :] = nn(k_turned[...], d_scores).T

        @pl.loop(0, 4)
        def _(i):
            at = pl.ds(pl.multiple_of(i * rows, rows), rows)
            for part, grad, marked in ((0, dq, q_marked), (1, dk, k_marked)):
                normed = marked[h, at, 0:HD].astype(jnp.float32)
                got = grad[at, :]
                inner = jnp.mean(got * normed, axis=-1, keepdims=True)
                d_proj[at, part * HD:(part + 1) * HD] = (
                    (factors[part, h, at, :] * scale) * (got - normed * inner)).astype(jnp.bfloat16)
            d_proj[at, 2 * HD:3 * HD] = dv[at, :].astype(jnp.bfloat16)

    out_slab = Slab(HEADS)
    slabs = [Slab(h) for h in range(HEADS)]
    weight_grads(HEADS, d_full, mixed)
    out_slab.far_start()

    @pl.loop(0, 4)
    def _(i):
        at = pl.ds(pl.multiple_of(i * rows, rows), rows)
        got = nn(d_full[at, :], w_out[...])
        for h in range(HEADS):
            d_out[at, h * HD:(h + 1) * HD] = (got[:, h * HD:(h + 1) * HD] * inverse[h, at, :]).astype(jnp.bfloat16)

    head(0)
    out_slab.far_pass()
    weight_grads(0, x_full, d_proj)
    slabs[0].far_start()
    out_slab.near_start()
    head(1)
    slabs[0].far_pass()
    out_slab.near_pass()
    weight_grads(1, x_full, d_proj)
    slabs[1].far_start()
    slabs[0].near_start()
    out_slab.last_start()
    head(2)
    slabs[1].far_pass()
    slabs[0].near_pass()
    out_slab.end()
    weight_grads(2, x_full, d_proj)
    slabs[2].far_start()
    slabs[1].near_start()
    slabs[0].last_start()
    slabs[2].far_pass()
    slabs[1].near_pass()
    slabs[0].end()
    slabs[2].near_start()
    slabs[1].last_start()
    slabs[2].near_pass()
    slabs[1].end()
    slabs[2].last_start()
    slabs[2].end()
    copies.finish()


def backward(d_full, x_full, w_out, q_marked, k_marked, v_half, factors, inverse, mixed):
    group_rows, width = x_full.shape
    half = lambda *lead: pltpu.VMEM((SLABS, 2, *lead, 48, 3 * HD), jnp.bfloat16)
    vmem = pl.BlockSpec(memory_space=pltpu.VMEM)
    qkv_sums, out_sums = pl.pallas_call(
        backward_kernel,
        out_shape=(
            jax.ShapeDtypeStruct((2, 48, QKV), jnp.float32),
            jax.ShapeDtypeStruct((2, 48, OUT), jnp.float32),
        ),
        in_specs=[vmem] * 9,
        out_specs=(vmem, vmem),
        scratch_shapes=[
            pltpu.VMEM((group_rows, OUT), jnp.bfloat16),
            pltpu.VMEM((HD, group_rows), jnp.bfloat16),
            pltpu.VMEM((group_rows, HD), jnp.float32),
            pltpu.VMEM((group_rows, HD), jnp.float32),
            pltpu.VMEM((group_rows, HD), jnp.float32),
            pltpu.VMEM((group_rows, 3 * HD), jnp.bfloat16),
            pltpu.VMEM((SLABS, 4, 4, 2, 2, 48, 3 * HD), jnp.bfloat16),
            half(6, 2, 2),
            half(2, 2, 2),
            half(4, 2),
            half(6),
            half(2),
            half(2),
            half(),
            pltpu.SemaphoreType.DMA((26 * SLABS,)),
            pltpu.SemaphoreType.DMA((26 * SLABS,)),
        ],
        compiler_params=pltpu.CompilerParams(collective_id=3, has_side_effects=True, vmem_limit_bytes=VMEM_LIMIT),
        name="backward_scatter",
    )(d_full, x_full, w_out.reshape(width, OUT), q_marked, k_marked, v_half, factors, inverse, mixed)
    return qkv_sums.reshape(96, QKV), out_sums.reshape(96, OUT)


def spread(block_of, rows, columns):
    source = jnp.repeat(block_of, 8) * 8 + jnp.tile(jnp.arange(8, dtype=jnp.int32), rows // 8)
    source = jnp.where(jnp.repeat(block_of, 8) < 0, -1, source)
    return (source[:, None] == jnp.arange(columns, dtype=jnp.int32)[None, :]).astype(jnp.bfloat16)


def per_device(clip_rows, velocity_target, plan, segment_ids, reward_levels, w_qkv, w_out):
    groups = lax.axis_size("dp")
    shards = lax.axis_size("seq")
    place = lax.axis_index("dp")
    shard = lax.axis_index("seq")
    crossed = shard // 2
    group = place ^ crossed
    rows_dev, width = clip_rows.shape
    counts = plan[place, shard]
    send_start = jnp.cumsum(counts) - counts

    def by_device(values):
        return jnp.where(crossed == 1, values.reshape(-1, 2)[:, ::-1].reshape(-1), values)

    counts, send_start = by_device(counts), by_device(send_start)
    slot_index = jnp.arange(CAP, dtype=jnp.int32)
    source_block = jnp.where(slot_index[None, :] < counts[:, None], send_start[:, None] + slot_index[None, :], -1).reshape(-1)
    pack = spread(source_block, rows_dev * CAP, rows_dev)

    def packed(source_rows):
        return jnp.dot(pack, source_rows, preferred_element_type=jnp.float32).astype(jnp.bfloat16).reshape(groups, CAP * 8, width)

    arriving = plan[:, shard, group]
    arriving_end = jnp.cumsum(arriving)
    slot_ids = jnp.arange(groups, dtype=jnp.int32)
    source_group = jnp.sum((arriving_end[None, :] <= slot_ids[:, None]).astype(jnp.int32), axis=1)
    arriving_start = (arriving_end - arriving)[source_group]
    flat_slot = source_group * CAP + slot_ids - arriving_start
    chosen = spread(flat_slot, rows_dev, rows_dev * CAP)

    segments = segment_ids.shape[1]
    labels = jnp.concatenate([segment_ids, jnp.pad(reward_levels, ((0, 0), (0, HD - reward_levels.shape[1])))], axis=1)
    labels = jnp.broadcast_to(labels, (8, segments + HD))
    return backward(*forward(packed(clip_rows), w_qkv, w_out, labels, chosen, pack, velocity_target))


def solution(mesh):
    return jax.shard_map(
        per_device,
        mesh=mesh,
        in_specs=(
            P(("dp", "seq"), None),
            P(("dp", "seq"), None),
            P(),
            P("dp", None),
            P("dp", None),
            P("dp", "seq"),
            P("dp", "seq"),
        ),
        out_specs=(P("dp", "seq"), P("dp", "seq")),
        check_vma=False,
    )
```

time: 327 us -> 303 us (0.927)
  Pallas kernels: 301 us -> 285 us
    pallas_call x2 -> x1, Pallas kernels: 213 us -> 198 us  [forward(): pl.pallas_call(forward_kernel, out_shape=tuple((jax.ShapeDtypeStruct(*sha...]
where the time goes in v4:
time: 303 us; the launch traced here: 300 us
  Pallas kernels  285 us (94%)
  local copies, waits for them, and re-layouts  9.16 us (3%)
  other arithmetic  3.2 us (1%)
    pallas_call x1, Pallas kernels, forward(): pl.pallas_call(forward_kernel, out_shape=tuple((jax.ShapeDtypeStruct(*sha...  198 us
    pallas_call x1, Pallas kernels, backward(): pl.pallas_call(backward_kernel, out_shape=(jax.ShapeDtypeStruct((2, 48, Q...  86.4 us

profile of v4, /device:TPU:16, one launch (start us, length us, event | category | flops | bytes accessed | tf_op | source)
XLA Modules:
  0.0 300.5 jit_solution(15597501454027486079)
XLA Ops:
  0.7 0.5 broadcast.92
  1.2 1.3 fusion.8
  2.5 0.1 reshape_squeeze.3
  2.6 0.1 rev.6
  2.7 0.1 reshape.157
  2.8 0.7 fusion.5
  3.5 1.6 fusion.7
  5.1 0.1 reduce.4
  5.3 0.1 convert_reduce_fusion
  5.4 0.7 gather_fusion
  6.1 0.1 add_select_fusion.1
  6.2 0.1 select_n.85
  6.3 0.1 copy.13
  6.4 0.1 reduce-window.13
  6.5 0.1 reduce.1
  6.6 0.1 reshape.158
  6.7 0.1 rev.7
  6.7 0.1 reshape.159
  6.9 0.1 fusion.4
  6.9 0.1 lt.72
  7.1 0.1 fusion.3
  7.1 0.1 mul.35
  7.2 0.6 broadcast_in_dim.47.labels
  7.9 0.1 add_select_fusion
  8.0 0.1 select_n.81
  8.0 0.8 fusion.1.chosen
  8.9 0.8 fusion.pack
  9.7 2.7 convolution_convert_fusion
  12.4 198.3 %forward_residual_gradient.1 = (bf16[1024,3072]{1,0:T(8,128)(2,1)}, bf16[1024,3072]{1,0:T(8,128)(2,1)}, bf16[4,4,2,2,48,384]{5,4,3,2,1,0:T(8,128)(2,1)}, bf16[3,...) custom-call(bf16[32,16,3072]{2,1,0:T(8,128)(2,1)} %bitcast.18, ...), custom_call_target="tpu_custom_call" | custom-call | tf_op jit(solution)/shard_map/forward_residual_gradient/pallas_call | solution.py:444
  210.7 86.4 %backward_scatter.1 = (f32[2,48,1152]{2,1,0:T(8,128)}, f32[2,48,384]{2,1,0:T(8,128)}) custom-call(bf16[1024,3072]{1,0:T(8,128)(2,1)} %get-tuple-element.13.d_full, bf16[1024,3072]{1,0:T(8,128)(2,1)} %get-tuple-element.14.x_full, bf16[3072,384]{1,0:T(8,128)(2,1)} %bitcast.19, bf16[3,1024,256]{2,1,0:T(8,128)(2,1)} %get-tuple-element.16.q_marked, ...), custom_call_target="tpu_custom_call" | custom-call | tf_op jit(solution)/shard_map/backward_scatter/pallas_call | solution.py:679
  297.1 1.8 copy.17
  298.9 1.6 copy.18
  (10 shorter events, 0.1 us)
Async XLA Ops:
  0.6 9.1 %copy-start = (bf16[256,3072]{1,0:T(8,128)(2,1)S(1)}, bf16[256,3072]{1,0:T(8,128)(2,1)}, u32[]{:S(2)}) copy-start(bf16[256,3072]{1,0:T(8,128)(2,1)} %param.7) | copy-start | bytes 4718596

commit v5 on v4

--- a/solution.py
+++ b/solution.py
@@ -73,6 +73,8 @@
 
 def dp_peer(place, k, sign):
     z, x, y, a, c = place
+    k = (k * 13) % 32
+    sign = sign * (1 - 2 * c)
     dz, dx, dy = k // 8, (k // 2) % 4, k % 2
     return ((z + sign * dz + 4) % 4, (x + sign * dx + 4) % 4, (y + sign * dy + 2) % 2, a, c)
 
@@ -117,13 +119,13 @@
     return jnp.dot(left, right, preferred_element_type=jnp.float32)
 
 
-MOVES = 2
+MOVES = 3
 
 
 def forward_kernel(
-    packed, shard_qkv, shard_out, labels, chosen, pack, own_target,
+    plan, shard_qkv, shard_out, segments, levels, own_rows, own_target,
     d_full, x_out, w_out, q_out, k_out, v_out, factors_out, inverse_out, mixed_out,
-    w_full, x_full, received, packed_target, received_target, labels_there,
+    w_full, x_full, packed, received, received_target, labels, labels_there, pack, chosen,
     q_marked, k_marked, v_half, v_turned, factors, inverse, mixed,
     partial, target, from_core, from_chip, d_own,
     a2a_send, a2a_recv, send_sem, recv_sem, local_sem,
@@ -154,7 +156,69 @@
     shards = [
         local_copy(shard_qkv.at[:, :, h * 3 * HD:(h + 1) * 3 * HD], w_full.at[h, z, x, y]) for h in range(HEADS)
     ] + [local_copy(shard_out, w_full.at[HEADS, z, x, y])]
-    own_block = local_copy(packed.at[dp], received.at[dp])
+    tile = width // MOVES
+
+    def iota(shape, axis):
+        return lax.broadcasted_iota(jnp.int32, shape, axis)
+
+    def one_where(condition):
+        return jnp.where(condition, 1.0, 0.0).astype(jnp.bfloat16)
+
+    shards_of, groups = 4, 32
+    group = dp + a * (1 - 2 * y)
+    plan_half = plan[...].astype(jnp.float32).astype(jnp.bfloat16)
+    before = one_where(iota((groups, groups), 0) < iota((groups, groups), 1))
+    counts = nn(one_where(iota((8, groups * shards_of), 1) == dp * shards_of + a * 2 + c), plan_half).astype(jnp.bfloat16)
+    starts = nn(counts, before).astype(jnp.bfloat16)
+    to_group = iota((rows * CAP, groups), 1)
+    to_group = to_group + a * (1 - 2 * (to_group & 1))
+    here = one_where((iota((rows * CAP, groups), 0) >> 4) == to_group)
+    of_row = iota((rows * CAP, 1), 0)
+    which = ((of_row >> 3) & 1).astype(jnp.float32)
+    source = (nt(here, starts)[:, 0:1] + which) * 8.0 + (of_row & 7).astype(jnp.float32)
+    source = jnp.where(which < nt(here, counts)[:, 0:1], source, -1.0)
+    pack[...] = one_where(iota((rows * CAP, rows), 1).astype(jnp.float32) == source)
+    arriving = nn(
+        one_where(iota((groups, groups * shards_of), 1) == iota((groups, groups * shards_of), 0) * shards_of + a * 2 + c), plan_half)
+    arriving = jnp.where(iota((groups, groups), 1) == group, arriving, 0.0).astype(jnp.bfloat16)
+    counts = nt(jnp.ones((8, groups), jnp.bfloat16), arriving).astype(jnp.bfloat16)
+    starts = nn(counts, before).astype(jnp.bfloat16)
+    there = one_where((iota((groups, rows * CAP), 1) >> 4) == iota((groups, rows * CAP), 0))
+    of_column = iota((1, rows * CAP), 1)
+    which = ((of_column >> 3) & 1).astype(jnp.float32)
+    slot = nn(starts, there)[0:1, :] + which
+    slot = jnp.where(which < nn(counts, there)[0:1, :], slot, -1.0)
+    place = slot * 8.0 + (of_column & 7).astype(jnp.float32)
+    chosen[...] = one_where(iota((rows, rows * CAP), 0).astype(jnp.float32) == place)
+
+    labels[:, 0:group_rows] = jnp.broadcast_to(segments[...], (8, group_rows))
+    lane = iota((8, HD), 1)
+    labels[:, group_rows:group_rows + HD] = jnp.where(lane == 0, levels[0:1, 0:1], jnp.where(lane == 1, levels[0:1, 1:2], 0))
+
+    def fill(src, chunk):
+        for low in range(chunk * tile, (chunk + 1) * tile, 512):
+            blocks = nn(pack[...], src[:, low:low + 512]).astype(jnp.bfloat16)
+            packed[:, :, low:low + 512] = blocks.reshape(packed.shape[0], packed.shape[1], 512)
+
+    def block_copy(chunk, k):
+        to = dp_peer(me, k, 1)
+        dst = received_target if chunk == MOVES else received
+        columns = slice(None) if chunk == MOVES else slice(chunk * tile, (chunk + 1) * tile)
+        return pltpu.make_async_remote_copy(
+            src_ref=packed.at[device(to)["dp"], :, columns],
+            dst_ref=dst.at[dp, :, columns],
+            send_sem=a2a_send.at[chunk, k],
+            recv_sem=a2a_recv.at[chunk, k],
+            device_id=device(to),
+            device_id_type=MESH,
+        )
+
+    def own_block_copy(chunk):
+        dst = received_target if chunk == MOVES else received
+        columns = slice(None) if chunk == MOVES else slice(chunk * tile, (chunk + 1) * tile)
+        return local_copy(packed.at[dp, :, columns], dst.at[dp, :, columns])
+
+    fill(own_rows, 0)
     for copy in shards:
         copy.wait()
     pl.semaphore_wait(barrier, 33)
@@ -162,36 +226,21 @@
     copies = Copies(send_sem, recv_sem)
     across = copies.start(w_full.at[:, z, x, y], w_full.at[:, z, x, y], moved(me, Y, 1))
     labels_across = copies.start(labels, labels_there, moved(me, Y, 1))
-
-    def block_copy(which, src, dst, k):
-        to = dp_peer(me, k, 1)
-        return pltpu.make_async_remote_copy(
-            src_ref=src.at[device(to)["dp"]],
-            dst_ref=dst.at[dp],
-            send_sem=a2a_send.at[which, k],
-            recv_sem=a2a_recv.at[which, k],
-            device_id=device(to),
-            device_id_type=MESH,
-        )
-
-    @pl.loop(1, 32)
-    def _(k):
-        block_copy(0, packed, received, k).start()
-
-    tile = 512
-
-    @pl.loop(0, width // tile)
-    def _(t):
-        columns = pl.ds(pl.multiple_of(t * tile, tile), tile)
-        blocks = nn(pack[...], own_target[:, columns]).astype(jnp.bfloat16)
-        packed_target[:, :, columns] = blocks.reshape(packed_target.shape[0], packed_target.shape[1], tile)
-
-    def select(src, dst):
-        @pl.loop(0, width // tile)
-        def _(t):
-            columns = pl.ds(pl.multiple_of(t * tile, tile), tile)
-            blocks = src[:, :, columns].reshape(rows * CAP, tile)
-            dst[:, columns] = nn(chosen[...], blocks).astype(jnp.bfloat16)
+    own_blocks = []
+    for chunk in range(MOVES):
+        if chunk:
+            fill(own_rows, chunk)
+
+        @pl.loop(1, 32)
+        def _(k):
+            block_copy(chunk, k).start()
+
+        own_blocks.append(own_block_copy(chunk))
+
+    def select(src, dst, at, chunk):
+        for low in range(chunk * tile, (chunk + 1) * tile, 512):
+            blocks = src[:, :, low:low + 512].reshape(rows * CAP, 512)
+            dst[at, low:low + 512] = nn(chosen[...], blocks).astype(jnp.bfloat16)
 
     def near(half):
         if half == 0:
@@ -230,22 +279,31 @@
         step = rows // chunks
         return pl.ds(pl.multiple_of(device(place)["seq"] * rows + chunk * step, step), step)
 
-    own_block.wait()
-
-    @pl.loop(1, 32)
-    def _(k):
-        block_copy(0, packed, received, k).wait_recv()
-
-    select(received, x_full.at[rows_of(me)])
-    x_chip = []
-    for chunk in range(MOVES):
-        at = rows_of(me, chunk, MOVES)
-        x_chip.append(copies.start(x_full.at[at], x_full.at[at], other_chip))
-    x_core = copies.start(x_full.at[rows_of(me)], x_full.at[rows_of(me)], other_core)
+    x_chip, x_core, x_passed = [], [], []
+
+    def x_arrive(chunk):
+        own_blocks[chunk].wait()
+
+        @pl.loop(1, 32)
+        def _(k):
+            block_copy(chunk, k).wait_recv()
+
+        at = rows_of(me)
+        select(received, x_full, at, chunk)
+        part = x_full.at[at, chunk * tile:(chunk + 1) * tile]
+        x_chip.append(copies.start(part, part, other_chip))
+        x_core.append(copies.start(part, part, other_core))
+
+    def x_pass(chunk):
+        x_chip[chunk].wait_recv()
+        part = x_full.at[rows_of(other_chip), chunk * tile:(chunk + 1) * tile]
+        x_passed.append(copies.start(part, part, other_core))
+
+    x_arrive(0)
     far_start(1)
 
     labels_across.wait_recv()
-    lane = lax.broadcasted_iota(jnp.int32, (rows, HD), 1)
+    lane = iota((rows, HD), 1)
     for i in range(group_rows // rows):
         at = slice(i * rows, (i + 1) * rows)
         segment = jnp.where(a == 1, labels_there[0:1, at], labels[0:1, at]).astype(jnp.float32)
@@ -283,41 +341,45 @@
         def _(i):
             attend(h, pl.ds(pl.multiple_of(i * rows, rows), rows))
 
-    x_passed = []
-
-    def x_pass(chunk):
-        x_chip[chunk].wait_recv()
-        at = rows_of(other_chip, chunk, MOVES)
-        x_passed.append(copies.start(x_full.at[at], x_full.at[at], other_core))
-
+    x_arrive(1)
+    x_pass(0)
     far_forward(0)
-    x_core.wait_recv()
+    x_arrive(2)
     far_wait(0)
     far_start(2)
+    far_forward(1)
+    x_pass(1)
+    for copy in x_core:
+        copy.wait_recv()
     project(0, a)
-    x_pass(0)
-    far_forward(1)
     far_wait(1)
     far_start(3)
     project(1, a)
     far_forward(2)
-    x_pass(1)
-    far_wait(2)
-    project(2, a)
-    far_forward(3)
-
-    @pl.loop(1, 32)
-    def _(k):
-        block_copy(1, packed_target, received_target, k).start()
-
-    own_block = local_copy(packed_target.at[dp], received_target.at[dp])
+    x_pass(2)
     for copy in x_passed:
         copy.wait_recv()
     outs = [local_copy(x_full, x_out)]
     project(0, 1 - a)
+    far_forward(3)
     attend_all(0)
+    for chunk in range(MOVES):
+        @pl.loop(1, 32)
+        def _(k):
+            block_copy(chunk, k).wait_send()
+
+    for chunk in range(MOVES):
+        fill(own_target, chunk)
+
+    @pl.loop(1, 32)
+    def _(k):
+        block_copy(MOVES, k).start()
+
+    own_block = own_block_copy(MOVES)
     project(1, 1 - a)
     attend_all(1)
+    far_wait(2)
+    project(2, a)
     project(2, 1 - a)
     for src, dst in ((q_marked, q_out), (k_marked, k_out), (v_half, v_out), (factors, factors_out)):
         outs.append(local_copy(src, dst))
@@ -361,9 +423,10 @@
 
     @pl.loop(1, 32)
     def _(k):
-        block_copy(1, packed_target, received_target, k).wait_recv()
-
-    select(received_target, target)
+        block_copy(MOVES, k).wait_recv()
+
+    for chunk in range(MOVES):
+        select(received_target, target, slice(None), chunk)
     own_lanes = rows_of(me)
     segment = jnp.where(a == 1, labels_there[0:1, own_lanes], labels[0:1, own_lanes]).astype(jnp.float32)
     first, second = (
@@ -397,17 +460,17 @@
 
     @pl.loop(1, 32)
     def _(k):
-        block_copy(0, packed, received, k).wait_send()
-        block_copy(1, packed_target, received_target, k).wait_send()
+        block_copy(MOVES, k).wait_send()
 
     for copy in outs:
         copy.wait()
     copies.finish()
 
 
-def forward(packed, shard_qkv, shard_out, labels, chosen, pack, own_target):
+def forward(plan, shard_qkv, shard_out, segments, levels, own_rows, own_target):
     rows, width = own_target.shape
     group_rows = rows * 4
+    blocks = (32, CAP * 8, width)
     vmem = pl.BlockSpec(memory_space=pltpu.VMEM)
     hbm = pl.BlockSpec(memory_space=pl.ANY)
     half, full = jnp.bfloat16, jnp.float32
@@ -423,10 +486,13 @@
     scratch = [
         ((SLABS, 4, 4, 2, 2, 48, 3 * HD), half),
         ((group_rows, width), half),
-        (packed.shape, half),
-        (packed.shape, half),
-        (packed.shape, half),
-        (labels.shape, labels.dtype),
+        (blocks, half),
+        (blocks, half),
+        (blocks, half),
+        ((8, group_rows + HD), jnp.int32),
+        ((8, group_rows + HD), jnp.int32),
+        ((rows * CAP, rows), half),
+        ((rows, rows * CAP), half),
         q_shape,
         k_shape,
         v_shape,
@@ -440,25 +506,27 @@
         ((rows, width), half),
         ((rows, width), half),
     ]
-    sems = 6 + 12 + 12 * SLABS + 2 * MOVES + 1 + 6 * CHUNKS
+    sems = 2 + 12 + 12 * SLABS + 3 * MOVES + 6 * CHUNKS
     return pl.pallas_call(
         forward_kernel,
         out_shape=tuple(
             jax.ShapeDtypeStruct(*shape)
             for shape in [((group_rows, width), half), ((group_rows, width), half), ((4, 4, 2, 2, 48, OUT), half)] + saved
         ),
-        in_specs=[hbm] * 3 + [vmem] * 4,
+        in_specs=[vmem] + [hbm] * 2 + [vmem] * 4,
         out_specs=(hbm,) * 9,
         scratch_shapes=[pltpu.VMEM(*shape) for shape in scratch] + [
-            pltpu.SemaphoreType.DMA((2, 32)),
-            pltpu.SemaphoreType.DMA((2, 32)),
+            pltpu.SemaphoreType.DMA((MOVES + 1, 32)),
+            pltpu.SemaphoreType.DMA((MOVES + 1, 32)),
             pltpu.SemaphoreType.DMA((sems,)),
             pltpu.SemaphoreType.DMA((sems,)),
-            pltpu.SemaphoreType.DMA((16,)),
+            pltpu.SemaphoreType.DMA((20,)),
         ],
         compiler_params=pltpu.CompilerParams(collective_id=2, has_side_effects=True, vmem_limit_bytes=VMEM_LIMIT),
         name="forward_residual_gradient",
-    )(packed, shard_qkv.reshape(2, 48, QKV), shard_out.reshape(2, 48, OUT), labels, chosen, pack, own_target)
+    )(
+        plan.reshape(-1, plan.shape[2]), shard_qkv.reshape(2, 48, QKV), shard_out.reshape(2, 48, OUT),
+        segments, levels, own_rows, own_target)
 
 
 def added(*values):
@@ -512,12 +580,16 @@
         out[index] = added(*[part[index] for part in parts]).astype(out.dtype)
 
 
-def backward_kernel(
-    d_full, x_full, w_out, q_marked, k_marked, v_half, factors, inverse, mixed,
-    qkv_sums, out_sums,
-    d_out, k_turned, dq, dk, dv, d_proj,
-    grads, got_far, sum_far, half_far, got_near, sum_near, half_near, got_last, send_sem, recv_sem,
-):
+def backward_kernel(*refs):
+    inputs, (qkv_sums, out_sums), held = refs[:9], refs[9:11], refs[11:20]
+    d_full, x_full, w_out, q_marked, k_marked, v_half, factors, inverse, mixed = held
+    (
+        d_out, k_turned, dq, dk, dv, d_proj,
+        grads, got_far, sum_far, half_far, got_near, sum_near, half_near, got_last, send_sem, recv_sem, local_sem,
+    ) = refs[20:]
+    loads = [pltpu.make_async_copy(inputs[i], held[i], local_sem.at[i]) for i in range(9)]
+    for i in (0, 8, 2, 7, 4, 3, 5, 1, 6):
+        loads[i].start()
     me = my_place()
     z, x, y, a, c = me
     greet([moved(me, Z, 1), moved(me, Z, -1), moved(me, X, 1), moved(me, X, -1), moved(me, Y, 1)])
@@ -630,8 +702,12 @@
 
     out_slab = Slab(HEADS)
     slabs = [Slab(h) for h in range(HEADS)]
+    loads[0].wait()
+    loads[8].wait()
     weight_grads(HEADS, d_full, mixed)
     out_slab.far_start()
+    for i in range(1, 8):
+        loads[i].wait()
 
     @pl.loop(0, 4)
     def _(i):
@@ -674,6 +750,7 @@
 
 def backward(d_full, x_full, w_out, q_marked, k_marked, v_half, factors, inverse, mixed):
     group_rows, width = x_full.shape
+    inputs = (d_full, x_full, w_out.reshape(width, OUT), q_marked, k_marked, v_half, factors, inverse, mixed)
     half = lambda *lead: pltpu.VMEM((SLABS, 2, *lead, 48, 3 * HD), jnp.bfloat16)
     vmem = pl.BlockSpec(memory_space=pltpu.VMEM)
     qkv_sums, out_sums = pl.pallas_call(
@@ -682,9 +759,9 @@
             jax.ShapeDtypeStruct((2, 48, QKV), jnp.float32),
             jax.ShapeDtypeStruct((2, 48, OUT), jnp.float32),
         ),
-        in_specs=[vmem] * 9,
+        in_specs=[pl.BlockSpec(memory_space=pl.ANY)] * 9,
         out_specs=(vmem, vmem),
-        scratch_shapes=[
+        scratch_shapes=[pltpu.VMEM(value.shape, value.dtype) for value in inputs] + [
             pltpu.VMEM((group_rows, OUT), jnp.bfloat16),
             pltpu.VMEM((HD, group_rows), jnp.bfloat16),
             pltpu.VMEM((group_rows, HD), jnp.float32),
@@ -701,53 +778,16 @@
             half(),
             pltpu.SemaphoreType.DMA((26 * SLABS,)),
             pltpu.SemaphoreType.DMA((26 * SLABS,)),
+            pltpu.SemaphoreType.DMA((9,)),
         ],
         compiler_params=pltpu.CompilerParams(collective_id=3, has_side_effects=True, vmem_limit_bytes=VMEM_LIMIT),
         name="backward_scatter",
-    )(d_full, x_full, w_out.reshape(width, OUT), q_marked, k_marked, v_half, factors, inverse, mixed)
+    )(*inputs)
     return qkv_sums.reshape(96, QKV), out_sums.reshape(96, OUT)
 
 
-def spread(block_of, rows, columns):
-    source = jnp.repeat(block_of, 8) * 8 + jnp.tile(jnp.arange(8, dtype=jnp.int32), rows // 8)
-    source = jnp.where(jnp.repeat(block_of, 8) < 0, -1, source)
-    return (source[:, None] == jnp.arange(columns, dtype=jnp.int32)[None, :]).astype(jnp.bfloat16)
-
-
 def per_device(clip_rows, velocity_target, plan, segment_ids, reward_levels, w_qkv, w_out):
-    groups = lax.axis_size("dp")
-    shards = lax.axis_size("seq")
-    place = lax.axis_index("dp")
-    shard = lax.axis_index("seq")
-    crossed = shard // 2
-    group = place ^ crossed
-    rows_dev, width = clip_rows.shape
-    counts = plan[place, shard]
-    send_start = jnp.cumsum(counts) - counts
-
-    def by_device(values):
-        return jnp.where(crossed == 1, values.reshape(-1, 2)[:, ::-1].reshape(-1), values)
-
-    counts, send_start = by_device(counts), by_device(send_start)
-    slot_index = jnp.arange(CAP, dtype=jnp.int32)
-    source_block = jnp.where(slot_index[None, :] < counts[:, None], send_start[:, None] + slot_index[None, :], -1).reshape(-1)
-    pack = spread(source_block, rows_dev * CAP, rows_dev)
-
-    def packed(source_rows):
-        return jnp.dot(pack, source_rows, preferred_element_type=jnp.float32).astype(jnp.bfloat16).reshape(groups, CAP * 8, width)
-
-    arriving = plan[:, shard, group]
-    arriving_end = jnp.cumsum(arriving)
-    slot_ids = jnp.arange(groups, dtype=jnp.int32)
-    source_group = jnp.sum((arriving_end[None, :] <= slot_ids[:, None]).astype(jnp.int32), axis=1)
-    arriving_start = (arriving_end - arriving)[source_group]
-    flat_slot = source_group * CAP + slot_ids - arriving_start
-    chosen = spread(flat_slot, rows_dev, rows_dev * CAP)
-
-    segments = segment_ids.shape[1]
-    labels = jnp.concatenate([segment_ids, jnp.pad(reward_levels, ((0, 0), (0, HD - reward_levels.shape[1])))], axis=1)
-    labels = jnp.broadcast_to(labels, (8, segments + HD))
-    return backward(*forward(packed(clip_rows), w_qkv, w_out, labels, chosen, pack, velocity_target))
+    return backward(*forward(plan, w_qkv, w_out, segment_ids, reward_levels, clip_rows, velocity_target))
 
 
 def solution(mesh):

time: 303 us -> 276 us (0.911)
  Pallas kernels: 285 us -> 271 us
  local copies, waits for them, and re-layouts: 9.16 us -> 3.38 us
  other arithmetic: 3.2 us -> 0 us
    pallas_call x1, Pallas kernels: 198 us -> 190 us  [forward(): pl.pallas_call(forward_kernel, out_shape=tuple((jax.ShapeDtypeStruct(*sha...]
    pallas_call x1, Pallas kernels: 86.4 us -> 80.7 us  [backward(): pl.pallas_call(backward_kernel, out_shape=(jax.ShapeDtypeStruct((2, 48, Q...]
    dynamic_slice x3 -> x0, local copies, waits for them, and re-layouts: 3.44 us -> none  [the longest x2 1.86 us: per_device(): counts = plan[place, shard]]
where the time goes in v5:
time: 276 us; the launch traced here: 275 us
  Pallas kernels  271 us (98%)
  local copies, waits for them, and re-layouts  3.38 us (1%)
    pallas_call x1, Pallas kernels, forward(): pl.pallas_call(forward_kernel, out_shape=tuple((jax.ShapeDtypeStruct(*sha...  190 us
    pallas_call x1, Pallas kernels, backward(): pl.pallas_call(backward_kernel, out_shape=(jax.ShapeDtypeStruct((2, 48, Q...  80.7 us

profile of v5, /device:TPU:16, one launch (start us, length us, event | category | flops | bytes accessed | tf_op | source)
XLA Modules:
  0.0 275.1 jit_solution(14940505551235110111)
XLA Ops:
  0.6 190.3 %forward_residual_gradient.1 = (bf16[1024,3072]{1,0:T(8,128)(2,1)}, bf16[1024,3072]{1,0:T(8,128)(2,1)}, bf16[4,4,2,2,48,384]{5,4,3,2,1,0:T(8,128)(2,1)}, bf16[3,...) custom-call(s32[128,32]{1,0:T(8,128)} %bitcast.11, ...), custom_call_target="tpu_custom_call" | custom-call | tf_op jit(solution)/shard_map/forward_residual_gradient/pallas_call | solution.py:510
  191.0 80.7 %backward_scatter.1 = (f32[2,48,1152]{2,1,0:T(8,128)}, f32[2,48,384]{2,1,0:T(8,128)}) custom-call(bf16[1024,3072]{1,0:T(8,128)(2,1)} %get-tuple-element.13.refs_0_, bf16[1024,3072]{1,0:T(8,128)(2,1)} %get-tuple-element.14.refs_1_, bf16[3072,384]{1,0:T(8,128)(2,1)} %bitcast.6, bf16[3,1024,256]{2,1,0:T(8,128)(2,1)} %get-tuple-element.16.refs_3_, ...), custom_call_target="tpu_custom_call" | custom-call | tf_op jit(solution)/shard_map/backward_scatter/pallas_call | solution.py:756
  271.7 1.8 copy.11
  273.5 1.6 copy.12

commit v6 on v5

--- a/solution.py
+++ b/solution.py
@@ -178,6 +178,61 @@
     source = (nt(here, starts)[:, 0:1] + which) * 8.0 + (of_row & 7).astype(jnp.float32)
     source = jnp.where(which < nt(here, counts)[:, 0:1], source, -1.0)
     pack[...] = one_where(iota((rows * CAP, rows), 1).astype(jnp.float32) == source)
+    labels[:, 0:group_rows] = jnp.broadcast_to(segments[...], (8, group_rows))
+    lane = iota((8, HD), 1)
+    labels[:, group_rows:group_rows + HD] = jnp.where(lane == 0, levels[0:1, 0:1], jnp.where(lane == 1, levels[0:1, 1:2], 0))
+
+    def fill(src, chunk):
+        for low in range(chunk * tile, (chunk + 1) * tile, 512):
+            blocks = nn(pack[...], src[:, low:low + 512]).astype(jnp.bfloat16)
+            packed[:, :, low:low + 512] = blocks.reshape(packed.shape[0], packed.shape[1], 512)
+
+    def block_copy(chunk, k):
+        to = dp_peer(me, k, 1)
+        dst = received_target if chunk == MOVES else received
+        columns = slice(None) if chunk == MOVES else slice(chunk * tile, (chunk + 1) * tile)
+        return pltpu.make_async_remote_copy(
+            src_ref=packed.at[device(to)["dp"], :, columns],
+            dst_ref=dst.at[dp, :, columns],
+            send_sem=a2a_send.at[chunk, k],
+            recv_sem=a2a_recv.at[chunk, k],
+            device_id=device(to),
+            device_id_type=MESH,
+        )
+
+    def own_block_copy(chunk):
+        dst = received_target if chunk == MOVES else received
+        columns = slice(None) if chunk == MOVES else slice(chunk * tile, (chunk + 1) * tile)
+        return local_copy(packed.at[dp, :, columns], dst.at[dp, :, columns])
+
+    fill(own_rows, 0)
+    for copy in shards:
+        copy.wait()
+    pl.semaphore_wait(barrier, 33)
+
+    copies = Copies(send_sem, recv_sem)
+    across = copies.start(w_full.at[0:HEADS, z, x, y], w_full.at[0:HEADS, z, x, y], moved(me, Y, 1))
+    labels_across = copies.start(labels, labels_there, moved(me, Y, 1))
+
+    def near_out(half):
+        columns = lambda which: pl.ds(0, 2 * HD) if which == half else pl.ds(2 * HD, HD)
+        if half == 0:
+            return lambda at, which: w_full.at[HEADS, at, x, y, 0, :, columns(which)]
+        return lambda at, which: w_full.at[HEADS, z, at, y, 1, :, columns(which)]
+
+    near_axis, far_axis = (Z, X), (X, Z)
+    out_sent = [ring_gather_start(copies, me, near_axis[half], near_out(half)) for half in (0, 1)]
+    own_blocks = []
+    for chunk in range(MOVES):
+        if chunk:
+            fill(own_rows, chunk)
+
+        @pl.loop(1, 32)
+        def _(k):
+            block_copy(chunk, k).start()
+
+        own_blocks.append(own_block_copy(chunk))
+
     arriving = nn(
         one_where(iota((groups, groups * shards_of), 1) == iota((groups, groups * shards_of), 0) * shards_of + a * 2 + c), plan_half)
     arriving = jnp.where(iota((groups, groups), 1) == group, arriving, 0.0).astype(jnp.bfloat16)
@@ -191,52 +246,6 @@
     place = slot * 8.0 + (of_column & 7).astype(jnp.float32)
     chosen[...] = one_where(iota((rows, rows * CAP), 0).astype(jnp.float32) == place)
 
-    labels[:, 0:group_rows] = jnp.broadcast_to(segments[...], (8, group_rows))
-    lane = iota((8, HD), 1)
-    labels[:, group_rows:group_rows + HD] = jnp.where(lane == 0, levels[0:1, 0:1], jnp.where(lane == 1, levels[0:1, 1:2], 0))
-
-    def fill(src, chunk):
-        for low in range(chunk * tile, (chunk + 1) * tile, 512):
-            blocks = nn(pack[...], src[:, low:low + 512]).astype(jnp.bfloat16)
-            packed[:, :, low:low + 512] = blocks.reshape(packed.shape[0], packed.shape[1], 512)
-
-    def block_copy(chunk, k):
-        to = dp_peer(me, k, 1)
-        dst = received_target if chunk == MOVES else received
-        columns = slice(None) if chunk == MOVES else slice(chunk * tile, (chunk + 1) * tile)
-        return pltpu.make_async_remote_copy(
-            src_ref=packed.at[device(to)["dp"], :, columns],
-            dst_ref=dst.at[dp, :, columns],
-            send_sem=a2a_send.at[chunk, k],
-            recv_sem=a2a_recv.at[chunk, k],
-            device_id=device(to),
-            device_id_type=MESH,
-        )
-
-    def own_block_copy(chunk):
-        dst = received_target if chunk == MOVES else received
-        columns = slice(None) if chunk == MOVES else slice(chunk * tile, (chunk + 1) * tile)
-        return local_copy(packed.at[dp, :, columns], dst.at[dp, :, columns])
-
-    fill(own_rows, 0)
-    for copy in shards:
-        copy.wait()
-    pl.semaphore_wait(barrier, 33)
-
-    copies = Copies(send_sem, recv_sem)
-    across = copies.start(w_full.at[:, z, x, y], w_full.at[:, z, x, y], moved(me, Y, 1))
-    labels_across = copies.start(labels, labels_there, moved(me, Y, 1))
-    own_blocks = []
-    for chunk in range(MOVES):
-        if chunk:
-            fill(own_rows, chunk)
-
-        @pl.loop(1, 32)
-        def _(k):
-            block_copy(chunk, k).start()
-
-        own_blocks.append(own_block_copy(chunk))
-
     def select(src, dst, at, chunk):
         for low in range(chunk * tile, (chunk + 1) * tile, 512):
             blocks = src[:, :, low:low + 512].reshape(rows * CAP, 512)
@@ -244,15 +253,15 @@
 
     def near(half):
         if half == 0:
-            return lambda at, which: w_full.at[:, at, x, which, 0]
-        return lambda at, which: w_full.at[:, z, at, which, 1]
+            return lambda at, which: w_full.at[0:HEADS, at, x, which, 0]
+        return lambda at, which: w_full.at[0:HEADS, z, at, which, 1]
 
     def far(s, half):
+        ys = pl.ds(y, 1) if s == HEADS else slice(None)
         if half == 0:
-            return lambda at, which: w_full.at[s, pl.ds(2 * which, 2), at, :, 0]
-        return lambda at, which: w_full.at[s, at, pl.ds(2 * which, 2), :, 1]
-
-    near_axis, far_axis = (Z, X), (X, Z)
+            return lambda at, which: w_full.at[s, pl.ds(2 * which, 2), at, ys, 0]
+        return lambda at, which: w_full.at[s, at, pl.ds(2 * which, 2), ys, 1]
+
     across.wait_recv()
     sent = [ring_gather_start(copies, me, near_axis[half], near(half)) for half in (0, 1)]
     rest = [ring_gather_forward(copies, me, near_axis[half], near(half), sent[half]) for half in (0, 1)]
@@ -273,6 +282,11 @@
             for copy in far_sent[s][half]:
                 copy.wait_recv()
 
+    out_rest = [ring_gather_forward(copies, me, near_axis[half], near_out(half), out_sent[half]) for half in (0, 1)]
+    for half in (0, 1):
+        for copy in out_rest[half]:
+            copy.wait_recv()
+    far_start(HEADS)
     far_start(0)
 
     def rows_of(place, chunk=0, chunks=1):
@@ -343,7 +357,11 @@
 
     x_arrive(1)
     x_pass(0)
+    far_forward(HEADS)
     far_forward(0)
+    far_wait(HEADS)
+    traded = [
+        copies.start(w_full.at[HEADS, :, :, y, half], w_full.at[HEADS, :, :, y, half], moved(me, Y, 1)) for half in (0, 1)]
     x_arrive(2)
     far_wait(0)
     far_start(2)
@@ -353,7 +371,6 @@
         copy.wait_recv()
     project(0, a)
     far_wait(1)
-    far_start(3)
     project(1, a)
     far_forward(2)
     x_pass(2)
@@ -361,7 +378,6 @@
         copy.wait_recv()
     outs = [local_copy(x_full, x_out)]
     project(0, 1 - a)
-    far_forward(3)
     attend_all(0)
     for chunk in range(MOVES):
         @pl.loop(1, 32)
@@ -383,7 +399,8 @@
     project(2, 1 - a)
     for src, dst in ((q_marked, q_out), (k_marked, k_out), (v_half, v_out), (factors, factors_out)):
         outs.append(local_copy(src, dst))
-    far_wait(3)
+    for copy in traded:
+        copy.wait_recv()
     outs.append(local_copy(w_full.at[HEADS], w_out))
 
     def block(place):
@@ -506,7 +523,7 @@
         ((rows, width), half),
         ((rows, width), half),
     ]
-    sems = 2 + 12 + 12 * SLABS + 3 * MOVES + 6 * CHUNKS
+    sems = 2 + 24 + 12 * SLABS + 2 + 3 * MOVES + 6 * CHUNKS
     return pl.pallas_call(
         forward_kernel,
         out_shape=tuple(

time: 276 us -> 274 us (level)
    pallas_call x1, Pallas kernels: 80.7 us -> 77.9 us  [backward(): pl.pallas_call(backward_kernel, out_shape=(jax.ShapeDtypeStruct((2, 48, Q...]
where the time goes in v6:
time: 274 us; the launch traced here: 273 us
  Pallas kernels  269 us (98%)
  local copies, waits for them, and re-layouts  3.38 us (1%)
    pallas_call x1, Pallas kernels, forward(): pl.pallas_call(forward_kernel, out_shape=tuple((jax.ShapeDtypeStruct(*sha...  191 us
    pallas_call x1, Pallas kernels, backward(): pl.pallas_call(backward_kernel, out_shape=(jax.ShapeDtypeStruct((2, 48, Q...  77.9 us

profile of v6, /device:TPU:16, one launch (start us, length us, event | category | flops | bytes accessed | tf_op | source)
XLA Modules:
  0.0 273.0 jit_solution(9394240077278443791)
XLA Ops:
  0.6 191.1 %forward_residual_gradient.1 = (bf16[1024,3072]{1,0:T(8,128)(2,1)}, bf16[1024,3072]{1,0:T(8,128)(2,1)}, bf16[4,4,2,2,48,384]{5,4,3,2,1,0:T(8,128)(2,1)}, bf16[3,...) custom-call(s32[128,32]{1,0:T(8,128)} %bitcast.11, ...), custom_call_target="tpu_custom_call" | custom-call | tf_op jit(solution)/shard_map/forward_residual_gradient/pallas_call | solution.py:527
  191.8 77.9 %backward_scatter.1 = (f32[2,48,1152]{2,1,0:T(8,128)}, f32[2,48,384]{2,1,0:T(8,128)}) custom-call(bf16[1024,3072]{1,0:T(8,128)(2,1)} %get-tuple-element.13.refs_0_, bf16[1024,3072]{1,0:T(8,128)(2,1)} %get-tuple-element.14.refs_1_, bf16[3072,384]{1,0:T(8,128)(2,1)} %bitcast.6, bf16[3,1024,256]{2,1,0:T(8,128)(2,1)} %get-tuple-element.16.refs_3_, ...), custom_call_target="tpu_custom_call" | custom-call | tf_op jit(solution)/shard_map/backward_scatter/pallas_call | solution.py:773
  269.6 1.8 copy.11
  271.4 1.6 copy.12

commit v7 on v6

--- a/solution.py
+++ b/solution.py
@@ -68,7 +68,7 @@
     barrier = pltpu.get_barrier_semaphore()
     for place in places:
         pl.semaphore_signal(barrier, inc=1, device_id=device(place), device_id_type=MESH)
-    pl.semaphore_wait(barrier, len(places))
+    return lambda: pl.semaphore_wait(barrier, len(places))
 
 
 def dp_peer(place, k, sign):
@@ -609,7 +609,7 @@
         loads[i].start()
     me = my_place()
     z, x, y, a, c = me
-    greet([moved(me, Z, 1), moved(me, Z, -1), moved(me, X, 1), moved(me, X, -1), moved(me, Y, 1)])
+    greeted = greet([moved(me, Z, 1), moved(me, Z, -1), moved(me, X, 1), moved(me, X, -1), moved(me, Y, 1)])
     copies = Copies(send_sem, recv_sem)
     far_axis, near_axis = (X, Z), (Z, X)
     group_rows, width = x_full.shape
@@ -722,6 +722,7 @@
     loads[0].wait()
     loads[8].wait()
     weight_grads(HEADS, d_full, mixed)
+    greeted()
     out_slab.far_start()
     for i in range(1, 8):
         loads[i].wait()

time: 274 us -> 274 us (level)
  no operation moved by 1% of the time
where the time goes in v7:
time: 274 us; the launch traced here: 273 us
  Pallas kernels  269 us (98%)
  local copies, waits for them, and re-layouts  3.38 us (1%)
    pallas_call x1, Pallas kernels, forward(): pl.pallas_call(forward_kernel, out_shape=tuple((jax.ShapeDtypeStruct(*sha...  191 us
    pallas_call x1, Pallas kernels, backward(): pl.pallas_call(backward_kernel, out_shape=(jax.ShapeDtypeStruct((2, 48, Q...  77.8 us

profile of v7, /device:TPU:16, one launch (start us, length us, event | category | flops | bytes accessed | tf_op | source)
XLA Modules:
  0.0 273.0 jit_solution(3418215608482124980)
XLA Ops:
  0.6 191.1 %forward_residual_gradient.1 = (bf16[1024,3072]{1,0:T(8,128)(2,1)}, bf16[1024,3072]{1,0:T(8,128)(2,1)}, bf16[4,4,2,2,48,384]{5,4,3,2,1,0:T(8,128)(2,1)}, bf16[3,...) custom-call(s32[128,32]{1,0:T(8,128)} %bitcast.11, ...), custom_call_target="tpu_custom_call" | custom-call | tf_op jit(solution)/shard_map/forward_residual_gradient/pallas_call | solution.py:527
  191.8 77.8 %backward_scatter.1 = (f32[2,48,1152]{2,1,0:T(8,128)}, f32[2,48,384]{2,1,0:T(8,128)}) custom-call(bf16[1024,3072]{1,0:T(8,128)(2,1)} %get-tuple-element.13.refs_0_, bf16[1024,3072]{1,0:T(8,128)(2,1)} %get-tuple-element.14.refs_1_, bf16[3072,384]{1,0:T(8,128)(2,1)} %bitcast.6, bf16[3,1024,256]{2,1,0:T(8,128)(2,1)} %get-tuple-element.16.refs_3_, ...), custom_call_target="tpu_custom_call" | custom-call | tf_op jit(solution)/shard_map/backward_scatter/pallas_call | solution.py:774
  269.6 1.8 copy.11
  271.4 1.6 copy.12
